TPU v7x, 32 devices: a whole 2x2x4 slice. The times are simulated.
32 devices in a mesh: row: 8 (over y, x, core), col: 4 (over z).
Axes of the slice: x: 2, y: 2, z: 4, core: 2. Of those that a mesh axis runs over, the one named last changes fastest.
Arguments:
- source_v: float32 [2, 4, 2560, 768], P(None, 'col', 'row'), may hold values from -6 to 6
- source_omega: float32 [2, 4, 2560, 768], P(None, 'col', 'row'), may hold values from -6 to 6
- forward_map: float32 [768, 768], P('col'), may hold values from -0.21875 to 0.21875
- back_maps: float32 [2, 768, 768], P(None, 'col'), may hold values from -0.21875 to 0.21875
- eigenvalues: float32 [768], replicated, may hold values from 0.02 to 4
- penalty: float32 [768, 3840], P('row'), may hold values from 0.05 to 4
Outputs:
- v_field: float32 [2, 4, 2560, 768], P(None, 'col', 'row')
- omega_field: float32 [2, 4, 2560, 768], P(None, 'col', 'row')
All inputs are finite; a program needn't handle non-finite values.
Results may differ from a plain program's by a relative error of at most 0.000098.
Values sent between devices are 32-bit elements; how exact they have to be, the bound alone decides.
A program may use at most 128 MiB of HBM per device.

v0:
```python
import math

import jax
import jax.numpy as jnp
from jax import lax
from jax.sharding import PartitionSpec as P


def helm_scale(eigen_part, flow_wave, span_wave):
    return 1.0 / (1.0 + eigen_part + 0.05 * (flow_wave * flow_wave + span_wave * span_wave))


def form_velocity(flow_wave, span_wave, derivative, vorticity):
    wave_sq = jnp.maximum(flow_wave * flow_wave + span_wave * span_wave, 1.0)
    along_real = (span_wave * vorticity[1] - flow_wave * derivative[1]) / wave_sq
    along_imag = (flow_wave * derivative[0] - span_wave * vorticity[0]) / wave_sq
    across_real = -(span_wave * derivative[1] + flow_wave * vorticity[1]) / wave_sq
    across_imag = (span_wave * derivative[0] + flow_wave * vorticity[0]) / wave_sq
    return (jnp.stack([along_real, along_imag]), jnp.stack([across_real, across_imag]))


def form_vorticity(flow_wave, span_wave, along, across):
    real_part = flow_wave * across[1] - span_wave * along[1]
    imag_part = span_wave * along[0] - flow_wave * across[0]
    return jnp.stack([real_part, imag_part])


def spanwise_tables(blocks_k, blocks_z, count_z):
    coarse_k = jnp.arange(blocks_k, dtype=jnp.int32)
    coarse_k = jnp.where(coarse_k < blocks_k // 2, coarse_k, coarse_k + blocks_z - blocks_k)
    coarse_z = jnp.arange(blocks_z, dtype=jnp.int32)
    fine_index = jnp.arange(128, dtype=jnp.int32)
    coarse_angle = (
        2.0
        * math.pi
        / blocks_z
        * (coarse_z[:, None] * coarse_k[None, :] % blocks_z).astype(jnp.float32)
    )
    twist_angle = (
        2.0
        * math.pi
        / count_z
        * (coarse_z[:, None] * fine_index[None, :] % count_z).astype(jnp.float32)
    )
    fine_angle = (
        2.0 * math.pi / 128 * (fine_index[:, None] * fine_index[None, :] % 128).astype(jnp.float32)
    )
    return (coarse_angle, twist_angle, fine_angle)


def block_table(cos_part, sin_part, axis_in):
    first = jnp.stack([cos_part, -sin_part], axis=axis_in)
    second = jnp.stack([sin_part, cos_part], axis=axis_in)
    return jnp.stack([first, second], axis=0)


def twist_apply(data, twist_cos, twist_sin):
    real_part = data[:, 0]
    imag_part = data[:, 1]
    return jnp.stack(
        [
            real_part * twist_cos - imag_part * twist_sin,
            real_part * twist_sin + imag_part * twist_cos,
        ],
        axis=1,
    )


def spanwise_pass(spanwise, factor_grid, count_z):
    count_kz = spanwise.shape[-1]
    blocks_k = count_kz // 128
    blocks_z = count_z // 128
    lead = spanwise.shape[:4]
    data = spanwise.reshape(lead + (blocks_k, 128))
    coarse_angle, twist_angle, fine_angle = spanwise_tables(blocks_k, blocks_z, count_z)
    coarse_cos, coarse_sin = (jnp.cos(coarse_angle), jnp.sin(coarse_angle))
    twist_cos, twist_sin = (jnp.cos(twist_angle), jnp.sin(twist_angle))
    fine_cos, fine_sin = (jnp.cos(fine_angle), jnp.sin(fine_angle))
    coarse_fwd = block_table(coarse_cos, coarse_sin, 1)
    fine_fwd = block_table(fine_cos, fine_sin, 1)
    fine_inv = block_table(fine_cos, -fine_sin, 1)
    coarse_inv = jnp.transpose(block_table(coarse_cos, -coarse_sin, 1), (0, 2, 1, 3)) / count_z
    data = jnp.einsum("cadk,fdxyks->fcxyas", coarse_fwd, data, precision=lax.Precision.HIGHEST)
    data = twist_apply(data, twist_cos, twist_sin)
    data = jnp.einsum("cnds,fdxyas->fcxyan", fine_fwd, data, precision=lax.Precision.HIGHEST)
    data = data * factor_grid
    data = jnp.einsum("ckdn,fdxyan->fcxyak", fine_inv, data, precision=lax.Precision.HIGHEST)
    data = twist_apply(data, twist_cos, -twist_sin)
    data = jnp.einsum("cdak,fdxyas->fcxyks", coarse_inv, data, precision=lax.Precision.HIGHEST)
    return data.reshape(lead + (count_kz,))


def shards(source_v, source_omega, forward_map, back_maps, eigenvalues, penalty):
    local_kx = source_v.shape[1]
    local_kz = source_v.shape[2]
    count_kz = local_kz * lax.axis_size("row")
    half_kz = count_kz // 2
    local_y = penalty.shape[0]
    count_z = penalty.shape[1]
    flow_index = lax.axis_index("col") * local_kx + jnp.arange(local_kx, dtype=jnp.int32)
    flow_wave = 0.5 * flow_index.astype(jnp.float32)
    span_index = lax.axis_index("row") * local_kz + jnp.arange(local_kz, dtype=jnp.int32)
    span_local = (
        jnp.where(span_index < half_kz, span_index, span_index - count_kz).astype(jnp.float32)
        * 8.0
        / half_kz
    )
    scaling = helm_scale(
        eigenvalues[None, None, :], flow_wave[:, None, None], span_local[None, :, None]
    )
    sources = jnp.stack([source_v, source_omega])
    flow_column = flow_wave[:, None, None]
    span_row = span_local[None, None, :]
    partial_coeffs = jnp.einsum(
        "fcxkn,jn->fcxkj",
        sources,
        lax.all_gather(forward_map, "col", axis=0, tiled=True),
        precision=lax.Precision.HIGHEST,
    )
    coeffs = partial_coeffs * scaling
    block_rows = lax.all_gather(back_maps, "col", axis=1, tiled=True)
    values = jnp.einsum("yj,fcxkj->fcxyk", block_rows[0], coeffs, precision=lax.Precision.HIGHEST)
    derivative = jnp.einsum(
        "yj,cxkj->cxyk", block_rows[1], coeffs[0], precision=lax.Precision.HIGHEST
    )
    along, across = form_velocity(flow_column, span_row, derivative, values[1])
    fields = jnp.stack([along, values[0], across])
    spanwise = lax.all_to_all(fields, "row", split_axis=3, concat_axis=4, tiled=True)
    factor_grid = jnp.transpose(
        (1.0 / (1.0 + penalty)).reshape(local_y, 128, count_z // 128), (0, 2, 1)
    )
    result = spanwise_pass(spanwise, factor_grid, count_z)
    returned = lax.all_to_all(result, "row", split_axis=4, concat_axis=3, tiled=True)
    v_part = returned[1]
    omega_part = form_vorticity(flow_column, span_row, returned[0], returned[2])
    return (jnp.transpose(v_part, (0, 1, 3, 2)), jnp.transpose(omega_part, (0, 1, 3, 2)))


def solution(mesh):
    placed = (
        P(None, "col", "row", None),
        P(None, "col", "row", None),
        P("col", None),
        P(None, "col", None),
        P(),
        P("row", None),
    )
    return jax.shard_map(
        shards,
        mesh=mesh,
        in_specs=placed,
        out_specs=(P(None, "col", "row", None), P(None, "col", "row", None)),
        check_vma=False,
    )
```

profile of v0, /device:TPU:0, one launch (start us, length us, event | category | flops | bytes accessed | tf_op | source)
XLA Modules:
  0.0 500.1 jit_solution(2554494599906409312)
XLA Ops:
  7.2 0.7 all-gather.3.cloned.1.call-update
  7.9 0.7 all-gather.5.cloned.1.call-update
  8.7 0.7 broadcast_add_fusion
  9.6 53.2 %all-gather.3.cloned.1.call-done = f32[768,768]{1,0:T(8,128)} async-done(((f32[192,768]{1,0:T(8,128)}), f32[768,768]{1,0:T(8,128)}) %all-gather.3.cloned.1.call-update) | async-done | bytes 2359312 | tf_op jit(solution)/shard_map/all_gather | solution.py:117
  62.8 13.7 %fusion.23 = f32[2,2,320,768]{3,2,1,0:T(8,128)} fusion(f32[768,768]{1,0:T(8,128)} %all-gather.3.cloned.1.call-done, f32[1,2,1,320,768]{4,3,1,0,2:T(8,128)} %bitcast.194, f32[1,2,1,320,768]{4,3,1,0,2:T(8,128)} %bitcast.195, f32[320,768]{1,0:T(8,128)S(1)} %add_divide_fusion.2), kind=kOutput, calls=%fused_computation.31 | convolution fusion | flops 9061662720 | bytes 11206656 | tf_op jit(solution)/shard_map/fcxkn,jn->fcxkj/dot_general | solution.py:114
  76.5 76.1 %all-gather.5.cloned.1.call-done = f32[2,768,768]{2,1,0:T(8,128)} async-done(((f32[2,192,768]{2,1,0:T(8,128)}), f32[2,768,768]{2,1,0:T(8,128)}) %all-gather.5.cloned.1.call-update) | async-done | bytes 4718608 | tf_op jit(solution)/shard_map/all_gather | solution.py:121
  152.6 13.3 %fusion.21 = f32[2,2,320,768]{3,2,1,0:T(8,128)S(1)} fusion(f32[2,2,320,768]{3,2,1,0:T(8,128)} %fusion.23, f32[2,768,768]{2,1,0:T(8,128)} %all-gather.5.cloned.1.call-done), kind=kOutput, calls=%fused_computation.29 | convolution fusion | flops 9059696640 | bytes 10223616 | tf_op jit(solution)/shard_map/yj,fcxkj->fcxyk/dot_general | solution.py:122
  166.0 5.5 %fusion.26 = f32[2,1,768,320]{2,3,0,1:T(8,128)S(1)} fusion(f32[2,768,768]{2,1,0:T(8,128)S(1)} %copy-done.2, f32[2,2,320,768]{3,2,1,0:T(8,128)S(1)} %copy-done), kind=kOutput, calls=%fused_computation.36 | convolution fusion | flops 4529848320 | bytes 6291456 | tf_op jit(solution)/shard_map/yj,cxkj->cxyk/dot_general | solution.py:123
  171.5 0.7 subtract_divide_fusion.1
  172.5 2.9 pad_maximum_fusion
  175.5 13.2 %copy.41 = f32[3,2,1,768,320]{4,1,0,2,3:T(2,128)} copy(f32[3,2,1,768,320]{3,4,1,0,2:T(8,128)} %pad_maximum_fusion) | data formatting | bytes 11796480 | tf_op jit(solution)/shard_map/stack | solution.py:127
  188.7 5.0 all-to-all-start
  193.8 1.8 copy.46
  195.6 1.6 reshape.757
  197.2 1.8 copy.47
  199.0 0.7 fusion.69
  199.7 0.7 fusion.59
  200.8 0.6 fusion.53
  201.4 0.3 fusion.47
  201.7 71.9 %all-to-all-done = f32[3,2,1,768,320]{4,1,0,2,3:T(2,128)} async-done(((f32[3,2,1,768,320]{4,1,0,2,3:T(2,128)}), f32[3,2,1,768,320]{4,1,0,2,3:T(2,128)}, u32[]{:S(2)}, u32[]{:S(2)}) %all-to-all-start) | async-done | bytes 5898272 | tf_op jit(solution)/shard_map/all_to_all | solution.py:128
  273.7 3.5 copy.42
  277.1 7.0 %copy.77 = f32[3,2,1,96,8,320]{5,4,1,3,0,2:T(8,128)} copy(f32[3,2,1,96,8,320]{5,3,4,1,0,2:T(8,128)S(1)} %bitcast.185) | data formatting | bytes 11796480 | tf_op jit(solution)/shard_map/reshape.27
  284.1 9.5 %reshape.764 = f32[3,2,96,20,128,1]{4,3,1,2,0,5:T(8,128)} reshape(f32[3,2,1,96,8,320]{5,4,1,3,0,2:T(8,128)} %copy.77) | data formatting | bytes 11796480 | tf_op jit(solution)/shard_map/reshape.27
  293.6 10.7 %fusion.13 = f32[3,2,1,96,30,128]{5,4,1,3,0,2:T(8,128)S(1)} fusion(f32[3,2,96,20,128,1]{4,3,1,2,0,5:T(8,128)} %reshape.764, f32[1,30,2,20]{1,3,2,0:T(8,128)S(1)} %get-tuple-element.27, f32[1,30,2,20]{1,3,2,0:T(8,128)S(1)} %get-tuple-element.30), kind=kOutput, calls=%fused_computation.23 | convolution fusion | flops 1061685632 | bytes 14755200 | tf_op jit(solution)/shard_map/cadk,fdxyks->fcxyas/dot_general | solution.py:83
  304.3 2.5 multiply_subtract_fusion.1
  306.8 1.6 maximum_bitcast_fusion
  308.3 13.7 %fusion.5 = f32[3,96,30,2,128,1]{4,1,5,3,2,0:T(8,128)S(1)} fusion(f32[3,2,96,30,128,1]{4,3,1,2,0,5:T(8,128)S(1)} %maximum_bitcast_fusion, f32[1,128,2,128]{3,1,2,0:T(8,128)S(1)} %get-tuple-element.21, f32[1,128,2,128]{3,1,2,0:T(8,128)S(1)} %get-tuple-element.24), kind=kOutput, calls=%fused_computation.9 | convolution fusion | flops 6794838016 | bytes 17956864 | tf_op jit(solution)/shard_map/cnds,fdxyas->fcxyan/dot_general | solution.py:85
  322.1 7.6 %fusion.16 = f32[3,96,30,2,128]{4,1,3,2,0:T(8,128)S(1)} fusion(f32[3,96,30,2,128,1]{4,1,5,3,2,0:T(8,128)S(1)} %fusion.5, f32[96,30,128]{2,0,1:T(8,128)S(1)} %copy-done.1, f32[1,128,2,128]{3,1,2,0:T(8,128)S(1)} %get-tuple-element.25, f32[1,128,2,128]{3,1,2,0:T(8,128)S(1)} %get-tuple-element.20), kind=kOutput, calls=%fused_computation.24 | convolution fusion | flops 6797049856 | bytes 19431424 | tf_op jit(solution)/shard_map/ckdn,fdxyan->fcxyak/dot_general | solution.py:87
  329.7 5.4 %copy.88 = f32[3,96,30,2,128]{4,2,3,1,0:T(8,128)S(1)} copy(f32[3,96,30,2,128]{4,1,3,2,0:T(8,128)S(1)} %fusion.16) | data formatting | bytes 17694720 | tf_op jit(solution)/shard_map/ckdn,fdxyan->fcxyak/dot_general | solution.py:87
  335.1 1.8 multiply_subtract_fusion
  336.9 10.1 %fusion.19 = f32[3,2,1,96,20,128]{5,4,1,3,0,2:T(8,128)} fusion(f32[3,1,1,96,30,128]{5,4,1,3,0,2:T(8,128)S(1)} %get-tuple-element.9, f32[3,1,1,96,30,128]{5,4,1,3,0,2:T(8,128)S(1)} %get-tuple-element.8, f32[1,30,2,20]{1,3,2,0:T(8,128)S(1)} %copy-done.8, f32[1,30,2,20]{1,3,2,0:T(8,128)S(1)} %copy-done.7), kind=kOutput, calls=%fused_computation.25 | convolution fusion | flops 1063899840 | bytes 14755200 | tf_op jit(solution)/shard_map/cdak,fdxyas->fcxyks/dot_general | solution.py:89
  347.0 10.4 %copy.84 = f32[3,2,1,96,20,128]{3,1,0,5,4,2:T(2,128)} copy(f32[3,2,1,96,20,128]{5,4,1,3,0,2:T(8,128)} %fusion.19) | data formatting | bytes 11796480 | tf_op jit(solution)/shard_map/reshape | solution.py:90
  357.4 94.0 %all_to_all.30 = f32[3,2,1,96,2560]{3,1,0,2,4:T(2,128)} all-to-all(f32[3,2,1,96,2560]{3,1,0,2,4:T(2,128)} %bitcast.181), channel_id=1, replica_groups=mesh['row'=8,'col'=4] {'row'}, dimensions={4} | all-to-all | bytes 11796480 | tf_op jit(solution)/shard_map/all_to_all | solution.py:133
  451.4 9.9 %copy.82 = f32[3,2,1,96,8,320]{5,4,3,1,0,2:T(8,128)} copy(f32[3,2,1,96,8,320]{3,1,0,5,4,2:T(2,128)} %bitcast.182) | data formatting | bytes 11796480 | tf_op jit(solution)/shard_map/all_to_all | solution.py:133
  461.2 4.0 fusion.81
  465.3 1.8 slice.103
  467.1 1.3 copy.54
  468.4 2.6 copy.55
  470.9 2.5 copy.53
  473.5 2.6 copy.56
  476.1 2.5 copy.57
  478.6 2.6 copy.58
  481.2 1.2 copy.59
  482.4 2.6 copy.60
  485.0 1.9 copy.52
  486.9 3.1 copy.61
  490.0 1.5 multiply_subtract_fusion.3
  491.4 1.4 maximum_bitcast_fusion.11
  (33 shorter events, 1.4 us)
Async XLA Ops:
  7.2 55.6 %all-gather.3.cloned.1.call-start = ((), (), s32[]{:S(2)}) async-start(), calls=%async_computation.2 | async-start | bytes 2949120 | tf_op jit(solution)/shard_map/all_gather | solution.py:117
  7.9 144.7 %all-gather.5.cloned.1.call-start = ((), (), s32[]{:S(2)}) async-start(), calls=%async_computation.3 | async-start | bytes 5898240 | tf_op jit(solution)/shard_map/all_gather | solution.py:121
  152.6 13.4 %copy-start = (f32[2,2,320,768]{3,2,1,0:T(8,128)S(1)}, f32[2,2,320,768]{3,2,1,0:T(8,128)}, u32[]{:S(2)}) copy-start(f32[2,2,320,768]{3,2,1,0:T(8,128)} %fusion.23) | copy-start | bytes 11796484
  152.6 13.4 %copy-start.2 = (f32[2,768,768]{2,1,0:T(8,128)S(1)}, f32[2,768,768]{2,1,0:T(8,128)}, u32[]{:S(2)}) copy-start(f32[2,768,768]{2,1,0:T(8,128)} %all-gather.5.cloned.1.call-done) | copy-start | bytes 14155780
  188.7 5.0 copy-start.6
  188.7 85.0 %all-to-all-start = ((f32[3,2,1,768,320]{4,1,0,2,3:T(2,128)}), f32[3,2,1,768,320]{4,1,0,2,3:T(2,128)}, u32[]{:S(2)}, u32[]{:S(2)}) async-start(f32[3,2,1,768,320]{4,1,0,2,3:T(2,128)} %copy.41), calls=%async_computation | async-start | bytes 14155776 | tf_op jit(solution)/shard_map/all_to_all | solution.py:128
  308.3 13.7 %copy-start.1 = (f32[96,30,128]{2,0,1:T(8,128)S(1)}, f32[96,30,128]{2,0,1:T(8,128)}, u32[]{:S(2)}) copy-start(f32[96,30,128]{2,0,1:T(8,128)} %copy.47) | copy-start | bytes 4423684
  329.7 5.4 %copy-start.9 = (f32[30,128]{1,0:T(8,128)S(1)}, f32[30,128]{1,0:T(8,128)}, u32[]{:S(2)}) copy-start(f32[30,128]{1,0:T(8,128)} %fusion.69) | copy-start | bytes 46084
  335.0 1.8 copy-start.7
  335.1 1.8 copy-start.8
  485.0 5.0 copy-start.3
  486.9 3.1 copy-start.4
  486.9 3.1 copy-start.5
Sparse Core Ops, SparseCore 0:
  9.6 53.1 all-gather.2
  64.4 88.2 all-gather.4
where the time goes:
time: 506 us; the launch traced here: 500 us
  waiting for transfers between devices  203 us (40%)
  blocking collectives  94 us (19%)
  local copies, waits for them, and re-layouts  88.7 us (18%)
  matrix products  74.6 us (15%)
  other arithmetic  20.4 us (4%)
  between operations  14.8 us (3%)
    all_to_all x1, blocking collectives, shards(): lax.all_to_all(result, 'row', split_axis=4, concat_axis=3, tiled=True)  94 us
    all_gather x1, waiting for transfers between devices, shards(): block_rows = lax.all_gather(back_maps, 'col', axis=1, tiled=True)  76.1 us
    all_to_all x1, waiting for transfers between devices, shards(): lax.all_to_all(fields, 'row', split_axis=3, concat_axis=4, tiled=True)  71.9 us
    all_gather x1, waiting for transfers between devices, shards(): lax.all_gather(forward_map, 'col', axis=0, tiled=True)  53.2 us
    another operation x2, local copies, waits for them, and re-layouts  16.4 us
    dot_general x1, matrix products, shards(): jnp.einsum('fcxkn,jn->fcxkj', sources, lax.all_gather(forward_map, 'col',...  13.7 us
    dot_general x1, matrix products, spanwise_pass(): jnp.einsum('cnds,fdxyas->fcxyan', fine_fwd, data, precision=lax.Precision...  13.7 us
    dot_general x1, matrix products, shards(): jnp.einsum('yj,fcxkj->fcxyk', block_rows[0], coeffs, precision=lax.Precis...  13.3 us
  transfers between devices with their start and end apart: 3, of which 3 were waited for; matrix products, arithmetic and copies ran while one was open for 5% of the time, Pallas kernels for 0%

commit v1 on v0

v1 whole, which is shorter than its diff:
```python
import functools
import math

import jax
import jax.numpy as jnp
import ml_dtypes
import numpy as np
from jax import lax
from jax.experimental import pallas as pl
from jax.experimental.pallas import tpu as pltpu
from jax.sharding import PartitionSpec as P

HIGH = lax.Precision.HIGH
BLOCKS = 8
ROWS = 8


def helm_scale(eigen_part, flow_wave, span_wave):
    return 1.0 / (1.0 + eigen_part + 0.05 * (flow_wave * flow_wave + span_wave * span_wave))


def split_table(table):
    high = table.astype(ml_dtypes.bfloat16)
    low = (table - high.astype(np.float64)).astype(ml_dtypes.bfloat16)
    return high, low


@functools.lru_cache
def spanwise_tables(block, count_z):
    coarse = count_z // block
    order = [a0 + 3 * a1 for a0 in range(3) for a1 in range(4)]
    r = np.arange(block)[:, None]
    b = np.arange(block)[None, :]
    tables = []
    for a in order:
        angle = 2.0 * math.pi * ((r * (a + coarse * b)) % count_z) / count_z
        cos, sin = np.cos(angle), np.sin(angle)
        tables.append(np.block([[cos, sin], [-sin, cos]]))
    high, low = split_table(np.stack(tables))
    weights = np.zeros((3, 16), np.float32)
    for a0 in range(3):
        for s0 in range(4):
            first = 2.0 * math.pi * s0 * a0 / 12
            second = 2.0 * math.pi * (s0 + 8) * a0 / 12
            weights[a0, 4 * s0 : 4 * s0 + 4] = (
                math.cos(first),
                math.sin(first),
                math.cos(second),
                math.sin(second),
            )
    return high, low, weights


def split_value(value):
    high = value.astype(jnp.bfloat16)
    low = (value - high.astype(jnp.float32)).astype(jnp.bfloat16)
    return high, low


def spanwise_kernel(weight_ref, flow_ref, x_ref, kz_ref, fac_ref, high_ref, low_ref, out_ref, u_ref, y_ref):
    a0 = pl.program_id(0)
    a1 = pl.program_id(1)
    rows, width = x_ref.shape[1], x_ref.shape[2]
    block = width // 2
    local_y = rows // 3
    sign = jnp.where(lax.broadcasted_iota(jnp.int32, (ROWS, width), 1) < block, -1.0, 1.0)

    def times_i(value):
        return sign * pltpu.roll(value, block, 1)

    def coefficients(s0):
        return [weight_ref[a0, 4 * s0 + p] for p in range(4)]

    @pl.when(a1 == 0)
    def _():
        @pl.loop(0, rows // ROWS)
        def _(step):
            at = pl.ds(pl.multiple_of(step * ROWS, ROWS), ROWS)
            z = []
            for s0 in range(4):
                c1, s1, c2, s2 = coefficients(s0)
                first, second = x_ref[s0, at, :], x_ref[s0 + 4, at, :]
                z.append(c1 * first + c2 * second + times_i(s1 * first + s2 * second))
            even, odd = z[0] + z[2], z[0] - z[2]
            total, turned = z[1] + z[3], times_i(z[1] - z[3])
            u_ref[0, at, :] = even + total
            u_ref[1, at, :] = odd + turned
            u_ref[2, at, :] = even - total
            u_ref[3, at, :] = odd - turned

    dot = functools.partial(lax.dot_general, preferred_element_type=jnp.float32)
    plain = (((1,), (0,)), ((), ()))
    flipped = (((1,), (1,)), ((), ()))
    table_high, table_low = high_ref[0], low_ref[0]

    for field in range(3):
        at = pl.ds(field * local_y, local_y)
        high, low = split_value(u_ref[a1, at, :])
        physical = dot(high, table_high, plain) + dot(high, table_low, plain) + dot(low, table_high, plain)
        high, low = split_value(physical * fac_ref[0])
        u_ref[a1, at, :] = (
            dot(high, table_high, flipped) + dot(high, table_low, flipped) + dot(low, table_high, flipped)
        )

    @pl.when(a1 == 3)
    def _():
        @pl.when(a0 == 0)
        def _():
            y_ref[...] = jnp.zeros_like(y_ref)

        @pl.loop(0, rows // ROWS)
        def _(step):
            at = pl.ds(pl.multiple_of(step * ROWS, ROWS), ROWS)
            even, odd = u_ref[0, at, :] + u_ref[2, at, :], u_ref[0, at, :] - u_ref[2, at, :]
            total, turned = u_ref[1, at, :] + u_ref[3, at, :], times_i(u_ref[1, at, :] - u_ref[3, at, :])
            q = [even + total, odd - turned, even - total, odd + turned]
            for s0 in range(4):
                c1, s1, c2, s2 = coefficients(s0)
                rotated = times_i(q[s0])
                y_ref[s0, at, :] += c1 * q[s0] - s1 * rotated
                y_ref[s0 + 4, at, :] += c2 * q[s0] - s2 * rotated

        @pl.when(a0 == 2)
        def _():
            flow_wave = flow_ref[0]

            @pl.loop(0, local_y // ROWS)
            def _(step):
                def at(field):
                    return pl.ds(pl.multiple_of(field * local_y + step * ROWS, ROWS), ROWS)

                for s in range(BLOCKS):
                    mixed = kz_ref[s : s + 1, :] * y_ref[s, at(0), :] - flow_wave * y_ref[s, at(2), :]
                    out_ref[s, 0, at(0), :] = y_ref[s, at(1), :]
                    out_ref[s, 1, at(0), :] = times_i(mixed)


def spanwise_pass(data, kz_rows, flow_wave, factor, count_z):
    _, rows, width = data.shape
    local_y = rows // 3
    high, low, weights = spanwise_tables(width // 2, count_z)
    whole = pl.BlockSpec(memory_space=pltpu.VMEM)
    scalars = pl.BlockSpec(memory_space=pltpu.SMEM)
    flops = 2 * 2 * 3 * 12 * rows * width * width
    return pl.pallas_call(
        spanwise_kernel,
        grid=(3, 4),
        out_shape=jax.ShapeDtypeStruct((BLOCKS, 2, local_y, width), jnp.float32),
        in_specs=[
            scalars,
            scalars,
            whole,
            whole,
            pl.BlockSpec((1, local_y, width), lambda i, j: (4 * i + j, 0, 0)),
            pl.BlockSpec((1, width, width), lambda i, j: (4 * i + j, 0, 0)),
            pl.BlockSpec((1, width, width), lambda i, j: (4 * i + j, 0, 0)),
        ],
        out_specs=whole,
        scratch_shapes=[
            pltpu.VMEM((4, rows, width), jnp.float32),
            pltpu.VMEM((BLOCKS, rows, width), jnp.float32),
        ],
        compiler_params=pltpu.CompilerParams(vmem_limit_bytes=44 * 2**20),
        cost_estimate=pl.CostEstimate(flops=flops, bytes_accessed=4 * 12 * width * width, transcendentals=0),
        name="spanwise",
    )(jnp.asarray(weights), flow_wave.reshape(1), data, kz_rows, factor, jnp.asarray(high), jnp.asarray(low))


def gather_rows(block, axis):
    share = lax.axis_size("row")
    extent = block.shape[axis]
    if extent % (8 * share):
        return lax.all_gather(block, "col", axis=axis, tiled=True)
    piece = extent // share
    own = lax.dynamic_slice_in_dim(block, lax.axis_index("row") * piece, piece, axis)
    return lax.all_gather(own, ("col", "row"), axis=axis, tiled=True)


def shards(source_v, source_omega, forward_map, back_maps, eigenvalues, penalty):
    _, local_kx, local_kz, count_y = source_v.shape
    assert local_kx == 1
    share = lax.axis_size("row")
    count_kz = local_kz * share
    half_kz = count_kz // 2
    local_y, count_z = penalty.shape
    block = count_kz // BLOCKS
    coarse = count_z // block
    assert coarse == 12 and share % BLOCKS == 0
    flow_wave = 0.5 * lax.axis_index("col").astype(jnp.float32)

    def wave_of(index):
        return jnp.where(index < half_kz, index, index - count_kz).astype(jnp.float32) * 8.0 / half_kz

    span_local = wave_of(lax.axis_index("row") * local_kz + jnp.arange(local_kz, dtype=jnp.int32))
    span = jnp.concatenate([span_local, span_local])[None, :]
    sign = jnp.where(jnp.arange(2 * local_kz) < local_kz, 1.0, -1.0)[None, :]
    scaling = helm_scale(eigenvalues[:, None], flow_wave, span)
    wave_sq = jnp.maximum(flow_wave * flow_wave + span * span, 1.0)

    forward = gather_rows(forward_map, 0)
    back = gather_rows(back_maps, 1)

    def rows_of(source):
        return source.reshape(2 * local_kz, count_y)

    def turned_rows(source):
        return jnp.concatenate([source[1, 0], source[0, 0]], axis=0)

    def coefficients(rows):
        return jnp.einsum("jn,kn->jk", forward, rows, precision=HIGH) * scaling

    def back_of(which, coeffs):
        return jnp.einsum("yj,jk->yk", back[which], coeffs, precision=HIGH)

    value = back_of(0, coefficients(rows_of(source_v)))
    derivative = back_of(1, coefficients(turned_rows(source_v)))
    vorticity = back_of(0, coefficients(turned_rows(source_omega)))
    along = sign * (span * vorticity - flow_wave * derivative) / wave_sq
    across = -sign * (span * derivative + flow_wave * vorticity) / wave_sq

    def by_owner(field):
        return field.reshape(share, local_y, 2 * local_kz)

    fields = jnp.stack([by_owner(along), by_owner(value), by_owner(across)], axis=1)
    arrived = lax.all_to_all(fields, "row", split_axis=0, concat_axis=0)
    merge = share // BLOCKS
    data = arrived
    if merge > 1:
        data = arrived.reshape(BLOCKS, merge, 3 * local_y, 2, local_kz)
        data = jnp.transpose(data, (0, 2, 3, 1, 4))
    data = data.reshape(BLOCKS, 3 * local_y, 2 * block)

    kz_rows = wave_of(jnp.arange(count_kz, dtype=jnp.int32)).reshape(BLOCKS, block)
    kz_rows = jnp.concatenate([kz_rows, kz_rows], axis=1)
    factor = jnp.transpose(penalty.reshape(local_y, block, coarse), (2, 0, 1))
    factor = factor.reshape(4, 3, local_y, block).transpose(1, 0, 2, 3).reshape(coarse, local_y, block)
    factor = (1.0 / count_z) / (1.0 + factor)
    factor = jnp.concatenate([factor, factor], axis=2)
    result = spanwise_pass(data, kz_rows, flow_wave, factor, count_z)
    if merge > 1:
        result = result.reshape(BLOCKS, 2, local_y, 2, merge, local_kz)
        result = jnp.transpose(result, (0, 4, 1, 2, 3, 5))
    result = result.reshape(share, 2, local_y, 2 * local_kz)
    returned = lax.all_to_all(result, "row", split_axis=0, concat_axis=0)

    def placed(field):
        flat = returned[:, field].reshape(count_y, 2 * local_kz)
        return jnp.transpose(flat).reshape(2, 1, local_kz, count_y)

    return placed(0), placed(1)


def solution(mesh):
    placed = (
        P(None, "col", "row", None),
        P(None, "col", "row", None),
        P("col", None),
        P(None, "col", None),
        P(),
        P("row", None),
    )
    return jax.shard_map(
        shards,
        mesh=mesh,
        in_specs=placed,
        out_specs=(P(None, "col", "row", None), P(None, "col", "row", None)),
        check_vma=False,
    )
```

time: 506 us -> 373 us (0.74); the launches traced: 500 us -> 373 us
  Pallas kernels: 0 us -> 86.3 us
  local copies, waits for them, and re-layouts: 88.7 us -> 24.8 us
  matrix products: 74.6 us -> 25.9 us
  blocking collectives: 94 us -> 48.7 us
  waiting for transfers between devices: 203 us -> 166 us
  other arithmetic: 20.4 us -> 2.03 us
    pallas_call x0 -> x1, Pallas kernels: none -> 86.3 us  [spanwise_pass(): pl.pallas_call(spanwise_kernel, grid=(3, 4), out_shape=jax.ShapeDtypeStru...]
    dot_general x7 -> x6, matrix products: 74.6 us -> 25.9 us  [the longest x3 15.3 us: coefficients(): return jnp.einsum('jn,kn->jk', forward, rows, precision=HIGH) * scaling]
    all_to_all x1, blocking collectives: 94 us -> 48.7 us  [shards(): returned = lax.all_to_all(result, 'row', split_axis=0, concat_axis=0)]
    another operation x3 -> x1, local copies, waits for them, and re-layouts: 29.6 us -> 2.92 us  [shards(): jnp.stack([by_owner(along), by_owner(value), by_owner(across)], axis=1)]
    all_gather x2, waiting for transfers between devices: 129 us -> 107 us  [gather_rows(): return lax.all_gather(own, ('col', 'row'), axis=axis, tiled=True)]
    all_to_all x2 -> x0, local copies, waits for them, and re-layouts: 13.3 us -> none  [the longest x1 9.87 us: shards(): lax.all_to_all(result, 'row', split_axis=4, concat_axis=3, tiled=True)]
    all_to_all x1, waiting for transfers between devices: 71.9 us -> 58.7 us  [shards(): arrived = lax.all_to_all(fields, 'row', split_axis=0, concat_axis=0)]
    reshape x2 -> x0, local copies, waits for them, and re-layouts: 12 us -> none  [the longest x1 10.4 us: spanwise_pass(): return data.reshape(lead + (count_kz,))]
  transfers between devices with their start and end apart: 3 -> 3, of which waited for: 3 -> 3; matrix products, arithmetic and copies ran while one was open for 5% -> 8% of each run, Pallas kernels for 0% -> 0%
where the time goes in v1:
time: 373 us
  waiting for transfers between devices  166 us (45%)
  Pallas kernels  86.3 us (23%)
  blocking collectives  48.7 us (13%)
  matrix products  25.9 us (7%)
  local copies, waits for them, and re-layouts  24.8 us (7%)
  between operations  14.2 us (4%)
  starting transfers between devices  5.14 us (1%)
    all_gather x2, waiting for transfers between devices, gather_rows(): return lax.all_gather(own, ('col', 'row'), axis=axis, tiled=True)  107 us
    pallas_call x1, Pallas kernels, spanwise_pass(): pl.pallas_call(spanwise_kernel, grid=(3, 4), out_shape=jax.ShapeDtypeStru...  86.3 us
    all_to_all x1, waiting for transfers between devices, shards(): arrived = lax.all_to_all(fields, 'row', split_axis=0, concat_axis=0)  58.7 us
    all_to_all x1, blocking collectives, shards(): returned = lax.all_to_all(result, 'row', split_axis=0, concat_axis=0)  48.7 us
    dot_general x3, matrix products, coefficients(): return jnp.einsum('jn,kn->jk', forward, rows, precision=HIGH) * scaling  15.3 us
    dot_general x3, matrix products, back_of(): return jnp.einsum('yj,jk->yk', back[which], coeffs, precision=HIGH)  10.5 us
    div x4, local copies, waits for them, and re-layouts, shards(): factor = 1.0 / count_z / (1.0 + factor)  7.55 us
  transfers between devices with their start and end apart: 3, of which 3 were waited for; matrix products, arithmetic and copies ran while one was open for 8% of the time, Pallas kernels for 0%

profile of v1, /device:TPU:0, one launch (start us, length us, event | category | flops | bytes accessed | tf_op | source)
XLA Modules:
  0.0 372.9 jit_solution(15523170319181853333)
XLA Ops:
  7.2 0.0 copy-start
  7.2 0.0 all-gather.5.cloned.1.call-start
  7.2 1.6 constant_dynamic-slice_fusion
  8.8 0.0 all-gather.5.cloned.1.call-update
  8.9 0.0 all-gather.3.cloned.1.call-start
  8.9 0.0 copy-done
  8.9 0.7 constant_dynamic-slice_fusion.1
  9.6 0.0 all-gather.3.cloned.1.call-update
  9.7 0.1 pad_maximum_fusion.3
  9.7 0.7 broadcast_add_fusion
  10.4 3.1 slice_bitcast_fusion.5
  13.5 0.0 copy-done.4
  13.5 1.1 slice_bitcast_fusion.3
  14.7 56.8 %all-gather.5.cloned.1.call-done = f32[768,768]{1,0:T(8,128)} async-done(((f32[24,768]{1,0:T(8,128)}), f32[768,768]{1,0:T(8,128)}) %all-gather.5.cloned.1.call-update) | async-done | bytes 2359312 | tf_op jit(solution)/shard_map/all_gather | solution.py:176
  71.5 6.7 %fusion.3 = f32[768,640]{1,0:T(8,128)} fusion(f32[768,768]{1,0:T(8,128)} %all-gather.5.cloned.1.call-done, f32[320,768]{1,0:T(8,128)} %get-tuple-element.9, f32[320,768]{1,0:T(8,128)} %get-tuple-element.8), kind=kOutput, calls=%fused_computation.6 | convolution fusion | flops 2265415680 | bytes 6291456 | tf_op jit(solution)/shard_map/jn,kn->jk/dot_general | solution.py:210
  78.1 0.0 copy-done.3
  78.1 0.0 copy-done.5
  78.1 4.3 %fusion.7 = f32[768,640]{1,0:T(8,128)} fusion(f32[768,768]{1,0:T(8,128)S(1)} %copy-done.3, f32[320,768]{1,0:T(8,128)S(1)} %copy-done.5, f32[320,768]{1,0:T(8,128)S(1)} %get-tuple-element.6), kind=kOutput, calls=%fused_computation.10 | convolution fusion | flops 2265415680 | bytes 6291456 | tf_op jit(solution)/shard_map/jn,kn->jk/dot_general | solution.py:210
  82.5 4.4 %fusion.43 = f32[768,640]{1,0:T(8,128)} fusion(f32[768,768]{1,0:T(8,128)S(1)} %copy-done.3, f32[640,768]{1,0:T(8,128)S(1)} %bitcast.50), kind=kOutput, calls=%fused_computation.61 | convolution fusion | flops 2264924160 | bytes 6291456 | tf_op jit(solution)/shard_map/jn,kn->jk/dot_general | solution.py:210
  86.8 50.2 %all-gather.3.cloned.1.call-done = f32[2,768,768]{2,1,0:T(8,128)} async-done(((f32[2,24,768]{2,1,0:T(8,128)}), f32[2,768,768]{2,1,0:T(8,128)}) %all-gather.3.cloned.1.call-update) | async-done | bytes 4718608 | tf_op jit(solution)/shard_map/all_gather | solution.py:176
  137.0 0.0 copy-done.8
  137.0 1.7 slice-done.2
  138.7 3.5 fusion.16
  142.2 0.0 slice-done
  142.2 0.0 slice-done.1
  142.2 0.0 copy-done.7
  142.2 0.0 copy-start.6
  142.2 3.3 fusion.1
  145.5 0.0 copy-done.6
  145.5 3.7 multiply_divide_fusion.1
  149.3 0.4 pad_maximum_fusion
  149.7 2.9 copy.20
  152.6 5.1 %all-to-all-start = ((f32[8,3,96,640]{3,2,1,0:T(8,128)}), f32[8,3,96,640]{3,2,1,0:T(8,128)}, u32[]{:S(2)}, u32[]{:S(2)}) async-start(f32[8,3,96,640]{3,2,1,0:T(8,128)} %copy.20), calls=%async_computation | async-start | bytes 11796480 | tf_op jit(solution)/shard_map/all_to_all | solution.py:225
  157.7 0.0 copy-done.9
  157.7 0.2 add_divide_fusion.1
  157.9 1.8 copy.21
  159.6 2.3 reshape.92
  161.9 2.0 copy.22
  163.9 1.6 copy.23
  165.5 0.1 pad_maximum_fusion.2.kz_ref
  165.5 0.6 pad_maximum_fusion.1.fac_ref
  166.1 58.7 %all-to-all-done = f32[8,3,96,640]{3,2,1,0:T(8,128)} async-done(((f32[8,3,96,640]{3,2,1,0:T(8,128)}), f32[8,3,96,640]{3,2,1,0:T(8,128)}, u32[]{:S(2)}, u32[]{:S(2)}) %all-to-all-start) | async-done | bytes 5898272 | tf_op jit(solution)/shard_map/all_to_all | solution.py:225
  224.8 0.0 copy-done.2
  224.8 86.3 %spanwise.1 = f32[8,2,96,640]{3,2,1,0:T(8,128)S(1)} custom-call(f32[3,16]{1,0:T(4,128)S(1)} %copy-done.2, f32[1]{0:T(128)} %bitcast.flow_ref, f32[8,288,640]{2,1,0:T(8,128)} %bitcast.13.x_ref, f32[8,640]{1,0:T(8,128)S(1)} %pad_maximum_fusion.2.kz_ref, f32[12,96,640]{2,1,0:T(8,128)S(1)} %pad_maximum_fusion.1.fac_ref, ...), custom_call_target="tpu_custom_call" | custom-call | flops 16986931200 | bytes 19660800 | tf_op jit(solution)/shard_map/spanwise/pallas_call | solution.py:145
  311.1 48.7 %all_to_all.10 = f32[8,2,96,640]{3,2,1,0:T(8,128)S(1)} all-to-all(f32[8,2,96,640]{3,2,1,0:T(8,128)S(1)} %spanwise.1), channel_id=1, replica_groups=mesh['row'=8,'col'=4] {'row'}, dimensions={0} | all-to-all | bytes 7864320 | tf_op jit(solution)/shard_map/all_to_all | solution.py:244
  359.9 1.5 fusion.42
  361.4 2.8 copy.24
  364.3 1.8 copy.25
  (16 shorter events, 0.0 us)
Async XLA Ops:
  7.2 1.8 copy-start
  7.2 64.3 %all-gather.5.cloned.1.call-start = ((), (), s32[]{:S(2)}) async-start(), calls=%async_computation.3 | async-start | bytes 2433024 | tf_op jit(solution)/shard_map/all_gather | solution.py:176
  8.9 128.1 %all-gather.3.cloned.1.call-start = ((), (), s32[]{:S(2)}) async-start(), calls=%async_computation.2 | async-start | bytes 4866048 | tf_op jit(solution)/shard_map/all_gather | solution.py:176
  10.4 3.1 copy-start.4
  71.5 6.7 %copy-start.3 = (f32[768,768]{1,0:T(8,128)S(1)}, f32[768,768]{1,0:T(8,128)}, u32[]{:S(2)}) copy-start(f32[768,768]{1,0:T(8,128)} %all-gather.5.cloned.1.call-done) | copy-start | bytes 7077892
  71.5 6.7 %copy-start.5 = (f32[320,768]{1,0:T(8,128)S(1)}, f32[320,768]{1,0:T(8,128)}, u32[]{:S(2)}) copy-start(f32[320,768]{1,0:T(8,128)} %get-tuple-element.7) | copy-start | bytes 2949124
  86.8 50.2 %copy-start.8 = (f32[768,640]{1,0:T(8,128)S(1)}, f32[768,640]{1,0:T(8,128)}, u32[]{:S(2)}) copy-start(f32[768,640]{1,0:T(8,128)} %fusion.43) | copy-start | bytes 5898244
  137.0 1.7 slice-start.2
  137.0 5.2 %slice-start = ((s8[4718592]{0:T(1024)(128)(4,1)}), s8[4194304]{0:T(1024)(128)(4,1)S(1)}, s32[]{:S(2)}) async-start(s8[4718592]{0:T(1024)(128)(4,1)} %bitcast.55), calls=%async_computation.4 | async-start | bytes 8388608
  138.7 3.5 slice-start.1
  138.7 3.5 copy-start.7
  142.2 3.3 copy-start.6
  152.6 5.1 %copy-start.9 = (f32[96,3840]{1,0:T(8,128)S(1)}, f32[96,3840]{1,0:T(8,128)}, u32[]{:S(2)}) copy-start(f32[96,3840]{1,0:T(8,128)} %param.14) | copy-start | bytes 4423684
  152.6 72.2 %all-to-all-start = ((f32[8,3,96,640]{3,2,1,0:T(8,128)}), f32[8,3,96,640]{3,2,1,0:T(8,128)}, u32[]{:S(2)}, u32[]{:S(2)}) async-start(f32[8,3,96,640]{3,2,1,0:T(8,128)} %copy.20), calls=%async_computation | async-start | bytes 11796480 | tf_op jit(solution)/shard_map/all_to_all | solution.py:225
  165.5 59.3 %copy-start.2 = (f32[3,16]{1,0:T(4,128)S(1)}, f32[3,16]{1,0:T(4,128)}, u32[]{:S(2)}) copy-start(f32[3,16]{1,0:T(4,128)} %constant.60.clone.weight_ref) | copy-start | bytes 580
  364.3 1.8 copy-start.1
Sparse Core Ops, SparseCore 0:
  11.5 59.9 all-gather.4
  74.4 62.5 all-gather.2

commit v2 on v1

--- a/solution.py
+++ b/solution.py
@@ -93,14 +93,13 @@
     flipped = (((1,), (1,)), ((), ()))
     table_high, table_low = high_ref[0], low_ref[0]
 
-    for field in range(3):
-        at = pl.ds(field * local_y, local_y)
-        high, low = split_value(u_ref[a1, at, :])
-        physical = dot(high, table_high, plain) + dot(high, table_low, plain) + dot(low, table_high, plain)
-        high, low = split_value(physical * fac_ref[0])
-        u_ref[a1, at, :] = (
-            dot(high, table_high, flipped) + dot(high, table_low, flipped) + dot(low, table_high, flipped)
-        )
+    def product(value, dims):
+        high, low = split_value(value)
+        both = dot(jnp.concatenate([high, low], axis=0), table_high, dims)
+        return both[:rows] + both[rows:] + dot(high, table_low, dims)
+
+    physical = product(u_ref[a1], plain).reshape(3, local_y, width)
+    u_ref[a1] = product((physical * fac_ref[0][None]).reshape(rows, width), flipped)
 
     @pl.when(a1 == 3)
     def _():
@@ -173,7 +172,10 @@
         return lax.all_gather(block, "col", axis=axis, tiled=True)
     piece = extent // share
     own = lax.dynamic_slice_in_dim(block, lax.axis_index("row") * piece, piece, axis)
-    return lax.all_gather(own, ("col", "row"), axis=axis, tiled=True)
+    column = lax.all_gather(own, "col", axis=axis, tiled=False)
+    everyone = lax.all_gather(column, "row", axis=axis + 1, tiled=False)
+    shape = block.shape[:axis] + (extent * lax.axis_size("col"),) + block.shape[axis + 1 :]
+    return everyone.reshape(shape)
 
 
 def shards(source_v, source_omega, forward_map, back_maps, eigenvalues, penalty):

time: 373 us -> 314 us (0.84)
  waiting for transfers between devices: 166 us -> 93.3 us
  blocking collectives: 48.7 us -> 82.6 us
  Pallas kernels: 86.3 us -> 66.7 us
    all_gather x2, waiting for transfers between devices: 107 us -> 34.5 us  [gather_rows(): everyone = lax.all_gather(column, 'row', axis=axis + 1, tiled=False)]
    all_gather x0 -> x2, blocking collectives: none -> 33.9 us  [gather_rows(): column = lax.all_gather(own, 'col', axis=axis, tiled=False)]
    pallas_call x1, Pallas kernels: 86.3 us -> 66.7 us  [spanwise_pass(): pl.pallas_call(spanwise_kernel, grid=(3, 4), out_shape=jax.ShapeDtypeStru...]
  transfers between devices with their start and end apart: 3 -> 3, of which waited for: 3 -> 3; matrix products, arithmetic and copies ran while one was open for 8% -> 9% of each run, Pallas kernels for 0% -> 0%
where the time goes in v2:
time: 314 us
  waiting for transfers between devices  93.3 us (30%)
  blocking collectives  82.6 us (26%)
  Pallas kernels  66.7 us (21%)
  matrix products  25.8 us (8%)
  local copies, waits for them, and re-layouts  24.6 us (8%)
  between operations  14.2 us (5%)
  starting transfers between devices  5.15 us (2%)
    pallas_call x1, Pallas kernels, spanwise_pass(): pl.pallas_call(spanwise_kernel, grid=(3, 4), out_shape=jax.ShapeDtypeStru...  66.7 us
    all_to_all x1, waiting for transfers between devices, shards(): arrived = lax.all_to_all(fields, 'row', split_axis=0, concat_axis=0)  58.7 us
    all_to_all x1, blocking collectives, shards(): returned = lax.all_to_all(result, 'row', split_axis=0, concat_axis=0)  48.7 us
    all_gather x2, waiting for transfers between devices, gather_rows(): everyone = lax.all_gather(column, 'row', axis=axis + 1, tiled=False)  34.5 us
    all_gather x2, blocking collectives, gather_rows(): column = lax.all_gather(own, 'col', axis=axis, tiled=False)  33.9 us
    dot_general x3, matrix products, coefficients(): return jnp.einsum('jn,kn->jk', forward, rows, precision=HIGH) * scaling  15.3 us
    dot_general x3, matrix products, back_of(): return jnp.einsum('yj,jk->yk', back[which], coeffs, precision=HIGH)  10.4 us
    div x4, local copies, waits for them, and re-layouts, shards(): factor = 1.0 / count_z / (1.0 + factor)  7.55 us
  transfers between devices with their start and end apart: 3, of which 3 were waited for; matrix products, arithmetic and copies ran while one was open for 9% of the time, Pallas kernels for 0%

profile of v2, /device:TPU:0, one launch (start us, length us, event | category | flops | bytes accessed | tf_op | source)
XLA Modules:
  0.0 313.7 jit_solution(6469796912275008473)
XLA Ops:
  7.2 0.0 copy-start
  7.2 0.0 copy-start.10
  7.2 0.0 all-gather.9.cloned.1.call-start
  7.2 1.0 constant_dynamic-slice_fusion
  8.2 16.3 %all-gather.2 = f32[96,768]{1,0:T(8,128)} all-gather(f32[24,768]{1,0:T(8,128)S(1)} %constant_dynamic-slice_fusion), channel_id=4, replica_groups=mesh['row'=8,'col'=4] {'col'}, dimensions={0}, use_global_device_ids=true | all-gather | bytes 368640 | tf_op jit(solution)/shard_map/all_gather | solution.py:175
  24.5 0.0 all-gather.9.cloned.1.call-update
  24.6 0.0 all-gather.7.cloned.1.call-start
  24.6 0.0 copy-done
  24.6 17.5 %all-gather = f32[2,96,768]{2,1,0:T(8,128)} all-gather(f32[2,24,768]{2,1,0:T(8,128)S(1)} %constant_dynamic-slice_fusion.1), channel_id=2, replica_groups=mesh['row'=8,'col'=4] {'col'}, dimensions={1}, use_global_device_ids=true | all-gather | bytes 737280 | tf_op jit(solution)/shard_map/all_gather | solution.py:175
  42.2 0.0 all-gather.7.cloned.1.call-update
  42.2 0.1 pad_maximum_fusion.3
  42.3 0.0 copy-done.10
  42.3 3.1 slice_bitcast_fusion.3
  45.5 0.0 copy-done.4
  45.5 1.1 slice_bitcast_fusion.1
  46.6 9.0 %all-gather.9.cloned.1.call-done = f32[4,192,768]{2,1,0:T(8,128)} async-done(((f32[4,24,768]{2,1,0:T(8,128)}), f32[4,192,768]{2,1,0:T(8,128)}) %all-gather.9.cloned.1.call-update) | async-done | bytes 2359312 | tf_op jit(solution)/shard_map/all_gather | solution.py:176
  55.6 6.7 %fusion = f32[768,640]{1,0:T(8,128)} fusion(f32[768,768]{1,0:T(8,128)} %bitcast.48, f32[320,768]{1,0:T(8,128)} %get-tuple-element.11, f32[320,768]{1,0:T(8,128)} %get-tuple-element.10), kind=kOutput, calls=%fused_computation.2 | convolution fusion | flops 2265415680 | bytes 6291456 | tf_op jit(solution)/shard_map/jn,kn->jk/dot_general | solution.py:212
  62.2 0.0 copy-done.3
  62.2 0.0 copy-done.5
  62.2 4.3 %fusion.4 = f32[768,640]{1,0:T(8,128)} fusion(f32[768,768]{1,0:T(8,128)S(1)} %bitcast.49, f32[320,768]{1,0:T(8,128)S(1)} %copy-done.5, f32[320,768]{1,0:T(8,128)S(1)} %get-tuple-element.8), kind=kOutput, calls=%fused_computation.6 | convolution fusion | flops 2265415680 | bytes 6291456 | tf_op jit(solution)/shard_map/jn,kn->jk/dot_general | solution.py:212
  66.6 4.3 %fusion.42 = f32[768,640]{1,0:T(8,128)} fusion(f32[768,768]{1,0:T(8,128)S(1)} %bitcast.50, f32[640,768]{1,0:T(8,128)S(1)} %bitcast.52), kind=kOutput, calls=%fused_computation.59 | convolution fusion | flops 2264924160 | bytes 6291456 | tf_op jit(solution)/shard_map/jn,kn->jk/dot_general | solution.py:212
  70.9 25.5 %all-gather.7.cloned.1.call-done = f32[2,4,192,768]{3,2,1,0:T(8,128)} async-done(((f32[2,4,24,768]{3,2,1,0:T(8,128)}), f32[2,4,192,768]{3,2,1,0:T(8,128)}) %all-gather.7.cloned.1.call-update) | async-done | bytes 4718608 | tf_op jit(solution)/shard_map/all_gather | solution.py:176
  96.4 2.7 fusion.40
  99.1 0.0 copy-done.7
  99.1 0.0 copy-start.8
  99.1 3.4 %fusion.13 = f32[768,640]{1,0:T(8,128)S(1)} fusion(f32[768,768]{1,0:T(8,128)S(1)} %bitcast.59, f32[768,640]{1,0:T(8,128)S(1)} %copy-done.7, f32[640]{0:T(1024)S(1)} %get-tuple-element.13, f32[768]{0:T(1024)S(1)} %broadcast_add_fusion), kind=kOutput, calls=%fused_computation.17 | convolution fusion | flops 2266398720 | bytes 6297088 | tf_op jit(solution)/shard_map/yj,jk->yk/dot_general | solution.py:215
  102.6 0.0 copy-done.8
  102.6 0.0 copy-start.6
  102.6 3.3 %fusion.15 = f32[8,1,96,640]{3,2,0,1:T(8,128)S(1)} fusion(f32[8,96,768]{2,1,0:T(8,128)S(1)} %bitcast.60, f32[768,640]{1,0:T(8,128)S(1)} %copy-done.8, f32[640]{0:T(1024)S(1)} %get-tuple-element.13, f32[768]{0:T(1024)S(1)} %broadcast_add_fusion), kind=kOutput, calls=%fused_computation.20 | convolution fusion | flops 2266398720 | bytes 6297088 | tf_op jit(solution)/shard_map/yj,jk->yk/dot_general | solution.py:215
  105.9 0.0 copy-done.6
  105.9 3.7 %multiply_divide_fusion.1 = (f32[768,640]{1,0:T(8,128)S(1)}, f32[768,640]{1,0:T(8,128)S(1)}) fusion(f32[768,640]{1,0:T(8,128)S(1)} %fusion.13, f32[640]{0:T(1024)S(1)} %get-tuple-element.14, f32[]{:T(128)} %mul_shard_map.3, f32[640]{0:T(1024)S(1)} %get-tuple-element.12, f32[640]{0:T(1024)S(1)} %get-tuple-element.15, f32[640]{0:T(1024)S(1)} %get-tuple-element.16, ...), kind=kOutput, calls=%fused_computation.14 | convolution fusion | flops 2271313920 | bytes 10239492 | tf_op jit(solution)/shard_map/yj,jk->yk/dot_general | solution.py:215
  109.6 0.4 pad_maximum_fusion
  110.0 2.9 copy.20
  113.0 5.1 %all-to-all-start = ((f32[8,3,96,640]{3,2,1,0:T(8,128)}), f32[8,3,96,640]{3,2,1,0:T(8,128)}, u32[]{:S(2)}, u32[]{:S(2)}) async-start(f32[8,3,96,640]{3,2,1,0:T(8,128)} %copy.20), calls=%async_computation | async-start | bytes 11796480 | tf_op jit(solution)/shard_map/all_to_all | solution.py:227
  118.0 0.0 copy-done.9
  118.0 0.2 add_divide_fusion.1
  118.3 1.8 copy.21
  120.0 2.3 reshape.101
  122.3 2.0 copy.22
  124.2 1.6 copy.23
  125.8 0.1 pad_maximum_fusion.2.kz_ref
  125.9 0.6 pad_maximum_fusion.1.fac_ref
  126.5 58.7 %all-to-all-done = f32[8,3,96,640]{3,2,1,0:T(8,128)} async-done(((f32[8,3,96,640]{3,2,1,0:T(8,128)}), f32[8,3,96,640]{3,2,1,0:T(8,128)}, u32[]{:S(2)}, u32[]{:S(2)}) %all-to-all-start) | async-done | bytes 5898272 | tf_op jit(solution)/shard_map/all_to_all | solution.py:227
  185.2 66.7 %spanwise.1 = f32[8,2,96,640]{3,2,1,0:T(8,128)S(1)} custom-call(f32[3,16]{1,0:T(4,128)S(1)} %copy-done.2, f32[1]{0:T(128)} %bitcast.flow_ref, f32[8,288,640]{2,1,0:T(8,128)} %bitcast.16.x_ref, f32[8,640]{1,0:T(8,128)S(1)} %pad_maximum_fusion.2.kz_ref, f32[12,96,640]{2,1,0:T(8,128)S(1)} %pad_maximum_fusion.1.fac_ref, ...), custom_call_target="tpu_custom_call" | custom-call | flops 16986931200 | bytes 19660800 | tf_op jit(solution)/shard_map/spanwise/pallas_call | solution.py:144
  251.9 48.7 %all_to_all.10 = f32[8,2,96,640]{3,2,1,0:T(8,128)S(1)} all-to-all(f32[8,2,96,640]{3,2,1,0:T(8,128)S(1)} %spanwise.1), channel_id=1, replica_groups=mesh['row'=8,'col'=4] {'row'}, dimensions={0} | all-to-all | bytes 7864320 | tf_op jit(solution)/shard_map/all_to_all | solution.py:246
  300.7 1.5 fusion.41
  302.2 2.8 copy.24
  305.1 1.8 copy.25
  (14 shorter events, 0.1 us)
Async XLA Ops:
  7.2 17.4 %copy-start = (f32[2,192,768]{2,1,0:T(8,128)S(1)}, f32[2,192,768]{2,1,0:T(8,128)}, u32[]{:S(2)}) copy-start(f32[2,192,768]{2,1,0:T(8,128)} %param.12) | copy-start | bytes 3538948
  7.2 35.2 %copy-start.10 = (f32[768]{0:T(1024)S(1)}, f32[768]{0:T(1024)}, u32[]{:S(2)}) copy-start(f32[768]{0:T(1024)} %param.13) | copy-start | bytes 9220
  7.2 48.4 %all-gather.9.cloned.1.call-start = ((), (), s32[]{:S(2)}) async-start(), calls=%async_computation.3 | async-start | bytes 2654208 | tf_op jit(solution)/shard_map/all_gather | solution.py:176
  24.6 71.9 %all-gather.7.cloned.1.call-start = ((), (), s32[]{:S(2)}) async-start(), calls=%async_computation.2 | async-start | bytes 5308416 | tf_op jit(solution)/shard_map/all_gather | solution.py:176
  42.3 3.1 copy-start.4
  55.6 6.7 %copy-start.3 = (f32[4,192,768]{2,1,0:T(8,128)S(1)}, f32[4,192,768]{2,1,0:T(8,128)}, u32[]{:S(2)}) copy-start(f32[4,192,768]{2,1,0:T(8,128)} %all-gather.9.cloned.1.call-done) | copy-start | bytes 7077892
  55.6 6.7 %copy-start.5 = (f32[320,768]{1,0:T(8,128)S(1)}, f32[320,768]{1,0:T(8,128)}, u32[]{:S(2)}) copy-start(f32[320,768]{1,0:T(8,128)} %get-tuple-element.9) | copy-start | bytes 2949124
  70.9 28.2 %copy-start.7 = (f32[768,640]{1,0:T(8,128)S(1)}, f32[768,640]{1,0:T(8,128)}, u32[]{:S(2)}) copy-start(f32[768,640]{1,0:T(8,128)} %fusion) | copy-start | bytes 5898244
  99.1 3.5 %copy-start.8 = (f32[768,640]{1,0:T(8,128)S(1)}, f32[768,640]{1,0:T(8,128)}, u32[]{:S(2)}) copy-start(f32[768,640]{1,0:T(8,128)} %fusion.42) | copy-start | bytes 5898244
  102.6 3.3 %copy-start.6 = (f32[768,640]{1,0:T(8,128)S(1)}, f32[768,640]{1,0:T(8,128)}, u32[]{:S(2)}) copy-start(f32[768,640]{1,0:T(8,128)} %fusion.4) | copy-start | bytes 5898244
  113.0 5.1 %copy-start.9 = (f32[96,3840]{1,0:T(8,128)S(1)}, f32[96,3840]{1,0:T(8,128)}, u32[]{:S(2)}) copy-start(f32[96,3840]{1,0:T(8,128)} %param.14) | copy-start | bytes 4423684
  113.0 72.2 %all-to-all-start = ((f32[8,3,96,640]{3,2,1,0:T(8,128)}), f32[8,3,96,640]{3,2,1,0:T(8,128)}, u32[]{:S(2)}, u32[]{:S(2)}) async-start(f32[8,3,96,640]{3,2,1,0:T(8,128)} %copy.20), calls=%async_computation | async-start | bytes 11796480 | tf_op jit(solution)/shard_map/all_to_all | solution.py:227
  125.9 59.3 %copy-start.2 = (f32[3,16]{1,0:T(4,128)S(1)}, f32[3,16]{1,0:T(4,128)}, u32[]{:S(2)}) copy-start(f32[3,16]{1,0:T(4,128)} %constant.60.clone.weight_ref) | copy-start | bytes 580
  305.1 1.8 copy-start.1
Sparse Core Ops, SparseCore 0:
  24.7 30.8 all-gather.8
  57.5 38.9 all-gather.6

commit v3 on v2

--- a/solution.py
+++ b/solution.py
@@ -73,7 +73,7 @@
 
     @pl.when(a1 == 0)
     def _():
-        @pl.loop(0, rows // ROWS)
+        @pl.loop(0, rows // ROWS, unroll=3)
         def _(step):
             at = pl.ds(pl.multiple_of(step * ROWS, ROWS), ROWS)
             z = []
@@ -107,7 +107,7 @@
         def _():
             y_ref[...] = jnp.zeros_like(y_ref)
 
-        @pl.loop(0, rows // ROWS)
+        @pl.loop(0, rows // ROWS, unroll=3)
         def _(step):
             at = pl.ds(pl.multiple_of(step * ROWS, ROWS), ROWS)
             even, odd = u_ref[0, at, :] + u_ref[2, at, :], u_ref[0, at, :] - u_ref[2, at, :]
@@ -165,17 +165,23 @@
     )(jnp.asarray(weights), flow_wave.reshape(1), data, kz_rows, factor, jnp.asarray(high), jnp.asarray(low))
 
 
-def gather_rows(block, axis):
+def gather_maps(forward_map, back_maps):
     share = lax.axis_size("row")
-    extent = block.shape[axis]
+    extent, count_y = forward_map.shape
     if extent % (8 * share):
-        return lax.all_gather(block, "col", axis=axis, tiled=True)
+        forward = lax.all_gather(forward_map, "col", axis=0, tiled=True)
+        return forward, lax.all_gather(back_maps, "col", axis=1, tiled=True)
     piece = extent // share
-    own = lax.dynamic_slice_in_dim(block, lax.axis_index("row") * piece, piece, axis)
-    column = lax.all_gather(own, "col", axis=axis, tiled=False)
-    everyone = lax.all_gather(column, "row", axis=axis + 1, tiled=False)
-    shape = block.shape[:axis] + (extent * lax.axis_size("col"),) + block.shape[axis + 1 :]
-    return everyone.reshape(shape)
+    start = lax.axis_index("row") * piece
+    own = [lax.dynamic_slice_in_dim(forward_map, start, piece, 0)[None]]
+    own.append(lax.dynamic_slice_in_dim(back_maps, start, piece, 1))
+    columns = lax.all_gather(jnp.concatenate(own, axis=0), "col", axis=1, tiled=False)
+
+    def everyone(part):
+        rows = lax.all_gather(part, "row", axis=2, tiled=False)
+        return rows.reshape(part.shape[0], extent * lax.axis_size("col"), count_y)
+
+    return everyone(columns[:1])[0], everyone(columns[1:])
 
 
 def shards(source_v, source_omega, forward_map, back_maps, eigenvalues, penalty):
@@ -199,8 +205,7 @@
     scaling = helm_scale(eigenvalues[:, None], flow_wave, span)
     wave_sq = jnp.maximum(flow_wave * flow_wave + span * span, 1.0)
 
-    forward = gather_rows(forward_map, 0)
-    back = gather_rows(back_maps, 1)
+    forward, back = gather_maps(forward_map, back_maps)
 
     def rows_of(source):
         return source.reshape(2 * local_kz, count_y)

time: 314 us -> 300 us (0.955)
  Pallas kernels: 66.7 us -> 47.6 us
  waiting for transfers between devices: 93.3 us -> 108 us
  blocking collectives: 82.6 us -> 71.1 us
    pallas_call x1, Pallas kernels: 66.7 us -> 47.6 us  [spanwise_pass(): pl.pallas_call(spanwise_kernel, grid=(3, 4), out_shape=jax.ShapeDtypeStru...]
    all_gather x2, waiting for transfers between devices: 34.5 us -> 48.8 us  [everyone(): rows = lax.all_gather(part, 'row', axis=2, tiled=False)]
    all_gather x2 -> x1, blocking collectives: 33.9 us -> 22.4 us  [gather_maps(): lax.all_gather(jnp.concatenate(own, axis=0), 'col', axis=1, tiled=False)]
  transfers between devices with their start and end apart: 3 -> 3, of which waited for: 3 -> 3; matrix products, arithmetic and copies ran while one was open for 9% -> 10% of each run, Pallas kernels for 0% -> 0%
where the time goes in v3:
time: 300 us
  waiting for transfers between devices  108 us (36%)
  blocking collectives  71.1 us (24%)
  Pallas kernels  47.6 us (16%)
  local copies, waits for them, and re-layouts  27.3 us (9%)
  matrix products  25.8 us (9%)
  between operations  14.2 us (5%)
  starting transfers between devices  5.15 us (2%)
    all_to_all x1, waiting for transfers between devices, shards(): arrived = lax.all_to_all(fields, 'row', split_axis=0, concat_axis=0)  58.7 us
    all_gather x2, waiting for transfers between devices, everyone(): rows = lax.all_gather(part, 'row', axis=2, tiled=False)  48.8 us
    all_to_all x1, blocking collectives, shards(): returned = lax.all_to_all(result, 'row', split_axis=0, concat_axis=0)  48.7 us
    pallas_call x1, Pallas kernels, spanwise_pass(): pl.pallas_call(spanwise_kernel, grid=(3, 4), out_shape=jax.ShapeDtypeStru...  47.6 us
    all_gather x1, blocking collectives, gather_maps(): lax.all_gather(jnp.concatenate(own, axis=0), 'col', axis=1, tiled=False)  22.4 us
    dot_general x3, matrix products, coefficients(): return jnp.einsum('jn,kn->jk', forward, rows, precision=HIGH) * scaling  15.3 us
    dot_general x3, matrix products, back_of(): return jnp.einsum('yj,jk->yk', back[which], coeffs, precision=HIGH)  10.4 us
    div x4, local copies, waits for them, and re-layouts, shards(): factor = 1.0 / count_z / (1.0 + factor)  7.55 us
  transfers between devices with their start and end apart: 3, of which 3 were waited for; matrix products, arithmetic and copies ran while one was open for 10% of the time, Pallas kernels for 0%

profile of v3, /device:TPU:0, one launch (start us, length us, event | category | flops | bytes accessed | tf_op | source)
XLA Modules:
  0.0 300.0 jit_solution(5166161614294752606)
XLA Ops:
  7.2 0.0 copy-start
  7.2 0.0 all-gather.8.cloned.1.call-start
  7.2 1.2 copy-done
  8.5 0.9 dynamic-slice_bitcast_fusion
  9.4 0.0 copy-start.10
  9.4 22.4 %all-gather = f32[3,96,768]{2,1,0:T(8,128)S(1)} all-gather(f32[3,24,768]{2,1,0:T(8,128)S(1)} %pad_maximum_fusion.2), channel_id=2, replica_groups=mesh['row'=8,'col'=4] {'col'}, dimensions={1}, use_global_device_ids=true | all-gather | bytes 1105920 | tf_op jit(solution)/shard_map/all_gather | solution.py:178
  31.8 0.7 slice.49
  32.5 0.0 all-gather.8.cloned.1.call-update
  32.5 0.0 all-gather.6.cloned.1.call-start
  32.6 0.8 slice.47
  33.4 0.0 all-gather.6.cloned.1.call-update
  33.5 0.1 pad_maximum_fusion.4
  33.6 0.0 copy-done.10
  33.6 3.1 %slice_bitcast_fusion.3 = (f32[320,768]{1,0:T(8,128)}, f32[320,768]{1,0:T(8,128)}) fusion(f32[2,1,320,768]{3,2,1,0:T(8,128)} %param.10), kind=kLoop, calls=%fused_computation.34 | loop fusion | bytes 3932160 | tf_op jit(solution)/shard_map/squeeze | solution.py:214
  36.7 0.0 copy-done.4
  36.7 1.1 slice_bitcast_fusion.1
  37.8 23.3 %all-gather.8.cloned.1.call-done = f32[1,4,192,768]{3,2,1,0:T(8,128)} async-done(((f32[1,4,24,768]{3,2,1,0:T(8,128)}), f32[1,4,192,768]{3,2,1,0:T(8,128)}) %all-gather.8.cloned.1.call-update) | async-done | bytes 2359312 | tf_op jit(solution)/shard_map/all_gather | solution.py:181
  61.1 6.7 %fusion = f32[768,640]{1,0:T(8,128)} fusion(f32[768,768]{1,0:T(8,128)} %bitcast.50, f32[320,768]{1,0:T(8,128)} %get-tuple-element.11, f32[320,768]{1,0:T(8,128)} %get-tuple-element.10), kind=kOutput, calls=%fused_computation.2 | convolution fusion | flops 2265415680 | bytes 6291456 | tf_op jit(solution)/shard_map/jn,kn->jk/dot_general | solution.py:217
  67.8 0.0 copy-done.3
  67.8 0.0 copy-done.5
  67.8 4.3 %fusion.4 = f32[768,640]{1,0:T(8,128)} fusion(f32[768,768]{1,0:T(8,128)S(1)} %bitcast.51, f32[320,768]{1,0:T(8,128)S(1)} %copy-done.5, f32[320,768]{1,0:T(8,128)S(1)} %get-tuple-element.8), kind=kOutput, calls=%fused_computation.6 | convolution fusion | flops 2265415680 | bytes 6291456 | tf_op jit(solution)/shard_map/jn,kn->jk/dot_general | solution.py:217
  72.1 4.3 %fusion.42 = f32[768,640]{1,0:T(8,128)} fusion(f32[768,768]{1,0:T(8,128)S(1)} %bitcast.52, f32[640,768]{1,0:T(8,128)S(1)} %bitcast.54), kind=kOutput, calls=%fused_computation.60 | convolution fusion | flops 2264924160 | bytes 6291456 | tf_op jit(solution)/shard_map/jn,kn->jk/dot_general | solution.py:217
  76.4 25.5 %all-gather.6.cloned.1.call-done = f32[2,4,192,768]{3,2,1,0:T(8,128)} async-done(((f32[2,4,24,768]{3,2,1,0:T(8,128)}), f32[2,4,192,768]{3,2,1,0:T(8,128)}) %all-gather.6.cloned.1.call-update) | async-done | bytes 4718608 | tf_op jit(solution)/shard_map/all_gather | solution.py:181
  102.0 2.7 fusion.40
  104.6 0.0 copy-done.7
  104.6 0.0 copy-start.8
  104.7 3.5 %fusion.13 = f32[768,640]{1,0:T(8,128)S(1)} fusion(f32[768,768]{1,0:T(8,128)S(1)} %bitcast.61, f32[768,640]{1,0:T(8,128)S(1)} %copy-done.7, f32[640]{0:T(1024)S(1)} %get-tuple-element.13, f32[768]{0:T(1024)S(1)} %broadcast_add_fusion), kind=kOutput, calls=%fused_computation.17 | convolution fusion | flops 2266398720 | bytes 6297088 | tf_op jit(solution)/shard_map/yj,jk->yk/dot_general | solution.py:220
  108.1 0.0 copy-done.8
  108.1 0.0 copy-start.6
  108.1 3.3 %fusion.15 = f32[8,1,96,640]{3,2,0,1:T(8,128)S(1)} fusion(f32[8,96,768]{2,1,0:T(8,128)S(1)} %bitcast.62, f32[768,640]{1,0:T(8,128)S(1)} %copy-done.8, f32[640]{0:T(1024)S(1)} %get-tuple-element.13, f32[768]{0:T(1024)S(1)} %broadcast_add_fusion), kind=kOutput, calls=%fused_computation.20 | convolution fusion | flops 2266398720 | bytes 6297088 | tf_op jit(solution)/shard_map/yj,jk->yk/dot_general | solution.py:220
  111.5 0.0 copy-done.6
  111.5 3.7 %multiply_divide_fusion.1 = (f32[768,640]{1,0:T(8,128)S(1)}, f32[768,640]{1,0:T(8,128)S(1)}) fusion(f32[768,640]{1,0:T(8,128)S(1)} %fusion.13, f32[640]{0:T(1024)S(1)} %get-tuple-element.14, f32[]{:T(128)} %mul_shard_map.3, f32[640]{0:T(1024)S(1)} %get-tuple-element.12, f32[640]{0:T(1024)S(1)} %get-tuple-element.15, f32[640]{0:T(1024)S(1)} %get-tuple-element.16, ...), kind=kOutput, calls=%fused_computation.14 | convolution fusion | flops 2271313920 | bytes 10239492 | tf_op jit(solution)/shard_map/yj,jk->yk/dot_general | solution.py:220
  115.2 0.4 pad_maximum_fusion
  115.6 2.9 copy.20
  118.5 5.1 %all-to-all-start = ((f32[8,3,96,640]{3,2,1,0:T(8,128)}), f32[8,3,96,640]{3,2,1,0:T(8,128)}, u32[]{:S(2)}, u32[]{:S(2)}) async-start(f32[8,3,96,640]{3,2,1,0:T(8,128)} %copy.20), calls=%async_computation | async-start | bytes 11796480 | tf_op jit(solution)/shard_map/all_to_all | solution.py:232
  123.6 0.2 add_divide_fusion.1
  123.8 1.8 copy.21
  125.6 2.3 reshape.97
  127.8 2.0 copy.22
  129.8 1.6 copy.23
  131.4 0.1 pad_maximum_fusion.3.kz_ref
  131.5 0.6 pad_maximum_fusion.1.fac_ref
  132.0 58.7 %all-to-all-done = f32[8,3,96,640]{3,2,1,0:T(8,128)} async-done(((f32[8,3,96,640]{3,2,1,0:T(8,128)}), f32[8,3,96,640]{3,2,1,0:T(8,128)}, u32[]{:S(2)}, u32[]{:S(2)}) %all-to-all-start) | async-done | bytes 5898272 | tf_op jit(solution)/shard_map/all_to_all | solution.py:232
  190.7 47.6 %spanwise.1 = f32[8,2,96,640]{3,2,1,0:T(8,128)S(1)} custom-call(f32[3,16]{1,0:T(4,128)S(1)} %copy-done.2, f32[1]{0:T(128)} %bitcast.flow_ref, f32[8,288,640]{2,1,0:T(8,128)} %bitcast.17.x_ref, f32[8,640]{1,0:T(8,128)S(1)} %pad_maximum_fusion.3.kz_ref, f32[12,96,640]{2,1,0:T(8,128)S(1)} %pad_maximum_fusion.1.fac_ref, ...), custom_call_target="tpu_custom_call" | custom-call | flops 16986931200 | bytes 19660800 | tf_op jit(solution)/shard_map/spanwise/pallas_call | solution.py:144
  238.3 48.7 %all_to_all.10 = f32[8,2,96,640]{3,2,1,0:T(8,128)S(1)} all-to-all(f32[8,2,96,640]{3,2,1,0:T(8,128)S(1)} %spanwise.1), channel_id=1, replica_groups=mesh['row'=8,'col'=4] {'row'}, dimensions={0} | all-to-all | bytes 7864320 | tf_op jit(solution)/shard_map/all_to_all | solution.py:251
  287.1 1.5 fusion.41
  288.6 2.8 copy.24
  291.4 1.8 copy.25
  (16 shorter events, 0.1 us)
Async XLA Ops:
  7.2 1.3 copy-start
  7.2 53.9 %all-gather.8.cloned.1.call-start = ((), (), s32[]{:S(2)}) async-start(), calls=%async_computation.3 | async-start | bytes 2654208 | tf_op jit(solution)/shard_map/all_gather | solution.py:181
  9.4 24.2 %copy-start.10 = (f32[768]{0:T(1024)S(1)}, f32[768]{0:T(1024)}, u32[]{:S(2)}) copy-start(f32[768]{0:T(1024)} %param.13) | copy-start | bytes 9220
  32.5 69.4 %all-gather.6.cloned.1.call-start = ((), (), s32[]{:S(2)}) async-start(), calls=%async_computation.2 | async-start | bytes 5308416 | tf_op jit(solution)/shard_map/all_gather | solution.py:181
  33.6 3.1 %copy-start.4 = (f32[2,1,320,768]{3,2,1,0:T(8,128)S(1)}, f32[2,1,320,768]{3,2,1,0:T(8,128)}, u32[]{:S(2)}) copy-start(f32[2,1,320,768]{3,2,1,0:T(8,128)} %param.9) | copy-start | bytes 5898244
  61.1 6.7 %copy-start.3 = (f32[1,4,192,768]{3,2,1,0:T(8,128)S(1)}, f32[1,4,192,768]{3,2,1,0:T(8,128)}, u32[]{:S(2)}) copy-start(f32[1,4,192,768]{3,2,1,0:T(8,128)} %all-gather.8.cloned.1.call-done) | copy-start | bytes 7077892
  61.1 6.7 %copy-start.5 = (f32[320,768]{1,0:T(8,128)S(1)}, f32[320,768]{1,0:T(8,128)}, u32[]{:S(2)}) copy-start(f32[320,768]{1,0:T(8,128)} %get-tuple-element.9) | copy-start | bytes 2949124
  76.4 28.2 %copy-start.7 = (f32[768,640]{1,0:T(8,128)S(1)}, f32[768,640]{1,0:T(8,128)}, u32[]{:S(2)}) copy-start(f32[768,640]{1,0:T(8,128)} %fusion) | copy-start | bytes 5898244
  104.6 3.5 %copy-start.8 = (f32[768,640]{1,0:T(8,128)S(1)}, f32[768,640]{1,0:T(8,128)}, u32[]{:S(2)}) copy-start(f32[768,640]{1,0:T(8,128)} %fusion.42) | copy-start | bytes 5898244
  108.1 3.3 %copy-start.6 = (f32[768,640]{1,0:T(8,128)S(1)}, f32[768,640]{1,0:T(8,128)}, u32[]{:S(2)}) copy-start(f32[768,640]{1,0:T(8,128)} %fusion.4) | copy-start | bytes 5898244
  118.5 5.1 %copy-start.9 = (f32[96,3840]{1,0:T(8,128)S(1)}, f32[96,3840]{1,0:T(8,128)}, u32[]{:S(2)}) copy-start(f32[96,3840]{1,0:T(8,128)} %param.14) | copy-start | bytes 4423684
  118.5 72.2 %all-to-all-start = ((f32[8,3,96,640]{3,2,1,0:T(8,128)}), f32[8,3,96,640]{3,2,1,0:T(8,128)}, u32[]{:S(2)}, u32[]{:S(2)}) async-start(f32[8,3,96,640]{3,2,1,0:T(8,128)} %copy.20), calls=%async_computation | async-start | bytes 11796480 | tf_op jit(solution)/shard_map/all_to_all | solution.py:232
  131.5 59.3 %copy-start.2 = (f32[3,16]{1,0:T(4,128)S(1)}, f32[3,16]{1,0:T(4,128)}, u32[]{:S(2)}) copy-start(f32[3,16]{1,0:T(4,128)} %constant.60.clone.weight_ref) | copy-start | bytes 580
  291.4 1.8 copy-start.1
Sparse Core Ops, SparseCore 0:
  32.6 28.4 all-gather.7
  63.0 38.9 all-gather.5

commit v4 on v3

--- a/solution.py
+++ b/solution.py
@@ -62,7 +62,8 @@
     a1 = pl.program_id(1)
     rows, width = x_ref.shape[1], x_ref.shape[2]
     block = width // 2
-    local_y = rows // 3
+    fields = x_ref.shape[1] // fac_ref.shape[1]
+    local_y = rows // fields
     sign = jnp.where(lax.broadcasted_iota(jnp.int32, (ROWS, width), 1) < block, -1.0, 1.0)
 
     def times_i(value):
@@ -98,7 +99,7 @@
         both = dot(jnp.concatenate([high, low], axis=0), table_high, dims)
         return both[:rows] + both[rows:] + dot(high, table_low, dims)
 
-    physical = product(u_ref[a1], plain).reshape(3, local_y, width)
+    physical = product(u_ref[a1], plain).reshape(fields, local_y, width)
     u_ref[a1] = product((physical * fac_ref[0][None]).reshape(rows, width), flipped)
 
     @pl.when(a1 == 3)
@@ -129,14 +130,16 @@
                     return pl.ds(pl.multiple_of(field * local_y + step * ROWS, ROWS), ROWS)
 
                 for s in range(BLOCKS):
-                    mixed = kz_ref[s : s + 1, :] * y_ref[s, at(0), :] - flow_wave * y_ref[s, at(2), :]
-                    out_ref[s, 0, at(0), :] = y_ref[s, at(1), :]
-                    out_ref[s, 1, at(0), :] = times_i(mixed)
+                    if fields == 1:
+                        out_ref[s, at(0), :] = y_ref[s, at(0), :]
+                    else:
+                        mixed = kz_ref[s : s + 1, :] * y_ref[s, at(0), :] - flow_wave * y_ref[s, at(1), :]
+                        out_ref[s, at(0), :] = times_i(mixed)
 
 
 def spanwise_pass(data, kz_rows, flow_wave, factor, count_z):
     _, rows, width = data.shape
-    local_y = rows // 3
+    local_y = factor.shape[1]
     high, low, weights = spanwise_tables(width // 2, count_z)
     whole = pl.BlockSpec(memory_space=pltpu.VMEM)
     scalars = pl.BlockSpec(memory_space=pltpu.SMEM)
@@ -144,7 +147,7 @@
     return pl.pallas_call(
         spanwise_kernel,
         grid=(3, 4),
-        out_shape=jax.ShapeDtypeStruct((BLOCKS, 2, local_y, width), jnp.float32),
+        out_shape=jax.ShapeDtypeStruct((BLOCKS, local_y, width), jnp.float32),
         in_specs=[
             scalars,
             scalars,
@@ -161,7 +164,7 @@
         ],
         compiler_params=pltpu.CompilerParams(vmem_limit_bytes=44 * 2**20),
         cost_estimate=pl.CostEstimate(flops=flops, bytes_accessed=4 * 12 * width * width, transcendentals=0),
-        name="spanwise",
+        name="spanwise_v" if rows == local_y else "spanwise_omega",
     )(jnp.asarray(weights), flow_wave.reshape(1), data, kz_rows, factor, jnp.asarray(high), jnp.asarray(low))
 
 
@@ -228,14 +231,19 @@
     def by_owner(field):
         return field.reshape(share, local_y, 2 * local_kz)
 
-    fields = jnp.stack([by_owner(along), by_owner(value), by_owner(across)], axis=1)
-    arrived = lax.all_to_all(fields, "row", split_axis=0, concat_axis=0)
     merge = share // BLOCKS
-    data = arrived
-    if merge > 1:
-        data = arrived.reshape(BLOCKS, merge, 3 * local_y, 2, local_kz)
-        data = jnp.transpose(data, (0, 2, 3, 1, 4))
-    data = data.reshape(BLOCKS, 3 * local_y, 2 * block)
+
+    def sent(*parts):
+        fields = jnp.stack([by_owner(part) for part in parts], axis=1)
+        data = lax.all_to_all(fields, "row", split_axis=0, concat_axis=0)
+        rows = len(parts) * local_y
+        if merge > 1:
+            data = data.reshape(BLOCKS, merge, rows, 2, local_kz)
+            data = jnp.transpose(data, (0, 2, 3, 1, 4))
+        return data.reshape(BLOCKS, rows, 2 * block)
+
+    data_v = sent(value)
+    data_omega = sent(along, across)
 
     kz_rows = wave_of(jnp.arange(count_kz, dtype=jnp.int32)).reshape(BLOCKS, block)
     kz_rows = jnp.concatenate([kz_rows, kz_rows], axis=1)
@@ -243,18 +251,18 @@
     factor = factor.reshape(4, 3, local_y, block).transpose(1, 0, 2, 3).reshape(coarse, local_y, block)
     factor = (1.0 / count_z) / (1.0 + factor)
     factor = jnp.concatenate([factor, factor], axis=2)
-    result = spanwise_pass(data, kz_rows, flow_wave, factor, count_z)
-    if merge > 1:
-        result = result.reshape(BLOCKS, 2, local_y, 2, merge, local_kz)
-        result = jnp.transpose(result, (0, 4, 1, 2, 3, 5))
-    result = result.reshape(share, 2, local_y, 2 * local_kz)
-    returned = lax.all_to_all(result, "row", split_axis=0, concat_axis=0)
-
-    def placed(field):
-        flat = returned[:, field].reshape(count_y, 2 * local_kz)
+
+    def finished(data):
+        result = spanwise_pass(data, kz_rows, flow_wave, factor, count_z)
+        if merge > 1:
+            result = result.reshape(BLOCKS, local_y, 2, merge, local_kz)
+            result = jnp.transpose(result, (0, 3, 1, 2, 4))
+        result = result.reshape(share, local_y, 2 * local_kz)
+        returned = lax.all_to_all(result, "row", split_axis=0, concat_axis=0)
+        flat = returned.reshape(count_y, 2 * local_kz)
         return jnp.transpose(flat).reshape(2, 1, local_kz, count_y)
 
-    return placed(0), placed(1)
+    return finished(data_v), finished(data_omega)
 
 
 def solution(mesh):

time: 300 us -> 272 us (0.907)
  blocking collectives: 71.1 us -> 22.4 us
  starting transfers between devices: 5.15 us -> 17 us
  Pallas kernels: 47.6 us -> 55.8 us
  waiting for transfers between devices: 108 us -> 100 us
  local copies, waits for them, and re-layouts: 27.3 us -> 30.5 us
    all_to_all x1 -> x0, blocking collectives: 48.7 us -> none  [shards(): returned = lax.all_to_all(result, 'row', split_axis=0, concat_axis=0)]
    all_to_all x1 -> x4, starting transfers between devices: 5.07 us -> 16.9 us  [the longest x2 8.51 us: sent(): data = lax.all_to_all(fields, 'row', split_axis=0, concat_axis=0)]
    all_to_all x1 -> x4, waiting for transfers between devices: 58.7 us -> 47 us  [the longest x2 24.6 us: sent(): data = lax.all_to_all(fields, 'row', split_axis=0, concat_axis=0)]
    pallas_call x1 -> x2, Pallas kernels: 47.6 us -> 55.8 us  [spanwise_pass(): pl.pallas_call(spanwise_kernel, grid=(3, 4), out_shape=jax.ShapeDtypeStru...]
    unnamed x22 -> x32, local copies, waits for them, and re-layouts: 1.26 us -> 7.48 us
    all_gather x2, waiting for transfers between devices: 48.8 us -> 53.2 us  [everyone(): rows = lax.all_gather(part, 'row', axis=2, tiled=False)]
  transfers between devices with their start and end apart: 3 -> 6, of which waited for: 3 -> 5; matrix products, arithmetic and copies ran while one was open for 10% -> 15% of each run, Pallas kernels for 0% -> 21%
where the time goes in v4:
time: 272 us; the launch traced here: 271 us
  waiting for transfers between devices  100 us (37%)
  Pallas kernels  55.8 us (21%)
  local copies, waits for them, and re-layouts  30.5 us (11%)
  matrix products  27.6 us (10%)
  blocking collectives  22.4 us (8%)
  starting transfers between devices  17 us (6%)
  between operations  14.3 us (5%)
  other arithmetic  3.11 us (1%)
    pallas_call x2, Pallas kernels, spanwise_pass(): pl.pallas_call(spanwise_kernel, grid=(3, 4), out_shape=jax.ShapeDtypeStru...  55.8 us
    all_gather x2, waiting for transfers between devices, everyone(): rows = lax.all_gather(part, 'row', axis=2, tiled=False)  53.2 us
    all_to_all x2, waiting for transfers between devices, sent(): data = lax.all_to_all(fields, 'row', split_axis=0, concat_axis=0)  24.6 us
    all_to_all x2, waiting for transfers between devices, finished(): returned = lax.all_to_all(result, 'row', split_axis=0, concat_axis=0)  22.4 us
    all_gather x1, blocking collectives, gather_maps(): lax.all_gather(jnp.concatenate(own, axis=0), 'col', axis=1, tiled=False)  22.4 us
    dot_general x3, matrix products, coefficients(): return jnp.einsum('jn,kn->jk', forward, rows, precision=HIGH) * scaling  16.1 us
    dot_general x3, matrix products, back_of(): return jnp.einsum('yj,jk->yk', back[which], coeffs, precision=HIGH)  11.5 us
    all_to_all x2, starting transfers between devices, sent(): data = lax.all_to_all(fields, 'row', split_axis=0, concat_axis=0)  8.51 us
  transfers between devices with their start and end apart: 6, of which 5 were waited for; matrix products, arithmetic and copies ran while one was open for 15% of the time, Pallas kernels for 21%

profile of v4, /device:TPU:0, one launch (start us, length us, event | category | flops | bytes accessed | tf_op | source)
XLA Modules:
  0.0 270.9 jit_solution(17631154150433750599)
XLA Ops:
  7.2 0.0 copy-start
  7.2 0.0 all-gather.8.cloned.1.call-start
  7.2 1.2 copy-done
  8.5 0.9 dynamic-slice_bitcast_fusion
  9.4 0.0 copy-start.15
  9.4 22.4 %all-gather = f32[3,96,768]{2,1,0:T(8,128)S(1)} all-gather(f32[3,24,768]{2,1,0:T(8,128)S(1)} %pad_maximum_fusion.2), channel_id=2, replica_groups=mesh['row'=8,'col'=4] {'col'}, dimensions={1}, use_global_device_ids=true | all-gather | bytes 1105920 | tf_op jit(solution)/shard_map/all_gather | solution.py:181
  31.8 0.7 slice.41
  32.5 0.0 all-gather.8.cloned.1.call-update
  32.5 0.0 all-gather.6.cloned.1.call-start
  32.6 0.9 slice.39
  33.5 0.0 all-gather.6.cloned.1.call-update
  33.5 0.1 pad_maximum_fusion.4
  33.6 3.1 %slice_bitcast_fusion.3 = (f32[320,768]{1,0:T(8,128)}, f32[320,768]{1,0:T(8,128)}) fusion(f32[2,1,320,768]{3,2,1,0:T(8,128)} %param.10), kind=kLoop, calls=%fused_computation.25 | loop fusion | bytes 3932160 | tf_op jit(solution)/shard_map/squeeze | solution.py:217
  36.7 1.1 slice_bitcast_fusion.1
  37.8 23.3 %all-gather.8.cloned.1.call-done = f32[1,4,192,768]{3,2,1,0:T(8,128)} async-done(((f32[1,4,24,768]{3,2,1,0:T(8,128)}), f32[1,4,192,768]{3,2,1,0:T(8,128)}) %all-gather.8.cloned.1.call-update) | async-done | bytes 2359312 | tf_op jit(solution)/shard_map/all_gather | solution.py:184
  61.1 6.6 %fusion = f32[768,640]{1,0:T(8,128)} fusion(f32[768,768]{1,0:T(8,128)} %bitcast.58, f32[320,768]{1,0:T(8,128)} %get-tuple-element.9, f32[320,768]{1,0:T(8,128)} %get-tuple-element.8), kind=kOutput, calls=%fused_computation.2 | convolution fusion | flops 2265415680 | bytes 6291456 | tf_op jit(solution)/shard_map/jn,kn->jk/dot_general | solution.py:220
  67.8 4.3 %fusion.41 = f32[768,640]{1,0:T(8,128)} fusion(f32[768,768]{1,0:T(8,128)S(1)} %bitcast.60, f32[640,768]{1,0:T(8,128)S(1)} %bitcast.62), kind=kOutput, calls=%fused_computation.59 | convolution fusion | flops 2264924160 | bytes 6291456 | tf_op jit(solution)/shard_map/jn,kn->jk/dot_general | solution.py:220
  72.1 29.9 %all-gather.6.cloned.1.call-done = f32[2,4,192,768]{3,2,1,0:T(8,128)} async-done(((f32[2,4,24,768]{3,2,1,0:T(8,128)}), f32[2,4,192,768]{3,2,1,0:T(8,128)}) %all-gather.6.cloned.1.call-update) | async-done | bytes 4718608 | tf_op jit(solution)/shard_map/all_gather | solution.py:184
  102.0 4.2 %fusion.40 = (f32[1,4,192,768]{3,2,1,0:T(8,128)}, f32[1,4,192,768]{3,2,1,0:T(8,128)S(1)}) fusion(f32[2,4,192,768]{3,2,1,0:T(8,128)} %all-gather.6.cloned.1.call-done), kind=kLoop, calls=%fused_computation.58 | loop fusion | bytes 9437184 | tf_op jit(solution)/shard_map/slice | solution.py:223
  106.1 1.4 copy-done.10
  107.5 4.5 %fusion.15 = f32[8,1,96,640]{3,2,1,0:T(8,128)} fusion(f32[8,96,768]{2,1,0:T(8,128)S(1)} %bitcast.68, f32[768,640]{1,0:T(8,128)S(1)} %copy-done.13, f32[640]{0:T(1024)S(1)} %get-tuple-element.11, f32[768]{0:T(1024)S(1)} %broadcast_add_fusion), kind=kOutput, calls=%fused_computation.20 | convolution fusion | flops 2266398720 | bytes 6297088 | tf_op jit(solution)/shard_map/yj,jk->yk/dot_general | solution.py:223
  112.0 3.8 %all-to-all-start = ((f32[8,1,96,640]{3,2,1,0:T(8,128)}), f32[8,1,96,640]{3,2,1,0:T(8,128)S(1)}, u32[]{:S(2)}, u32[]{:S(2)}) async-start(f32[8,1,96,640]{3,2,1,0:T(8,128)} %fusion.15), calls=%async_computation | async-start | bytes 3932160 | tf_op jit(solution)/shard_map/all_to_all | solution.py:238
  115.8 5.1 %fusion.4 = f32[768,640]{1,0:T(8,128)S(1)} fusion(f32[768,768]{1,0:T(8,128)} %bitcast.59, f32[320,768]{1,0:T(8,128)} %get-tuple-element.7, f32[320,768]{1,0:T(8,128)S(1)} %get-tuple-element.6), kind=kOutput, calls=%fused_computation.6 | convolution fusion | flops 2265415680 | bytes 6291456 | tf_op jit(solution)/shard_map/jn,kn->jk/dot_general | solution.py:220
  121.0 3.3 %fusion.12 = f32[768,640]{1,0:T(8,128)S(1)} fusion(f32[768,768]{1,0:T(8,128)S(1)} %bitcast.69, f32[768,640]{1,0:T(8,128)S(1)} %copy-done.12, f32[640]{0:T(1024)S(1)} %get-tuple-element.11, f32[768]{0:T(1024)S(1)} %broadcast_add_fusion), kind=kOutput, calls=%fused_computation.16 | convolution fusion | flops 2266398720 | bytes 6297088 | tf_op jit(solution)/shard_map/yj,jk->yk/dot_general | solution.py:223
  124.3 3.7 %multiply_divide_fusion.1 = (f32[768,640]{1,0:T(8,128)S(1)}, f32[768,640]{1,0:T(8,128)S(1)}) fusion(f32[768,640]{1,0:T(8,128)S(1)} %fusion.12, f32[640]{0:T(1024)S(1)} %get-tuple-element.12, f32[]{:T(128)} %mul_shard_map.3, f32[640]{0:T(1024)S(1)} %get-tuple-element.10, f32[640]{0:T(1024)S(1)} %get-tuple-element.13, f32[640]{0:T(1024)S(1)} %get-tuple-element.14, ...), kind=kOutput, calls=%fused_computation.13 | convolution fusion | flops 2271313920 | bytes 10239492 | tf_op jit(solution)/shard_map/yj,jk->yk/dot_general | solution.py:223
  128.0 2.2 pad_maximum_fusion
  130.2 10.6 %all-to-all-done = f32[8,1,96,640]{3,2,1,0:T(8,128)S(1)} async-done(((f32[8,1,96,640]{3,2,1,0:T(8,128)}), f32[8,1,96,640]{3,2,1,0:T(8,128)S(1)}, u32[]{:S(2)}, u32[]{:S(2)}) %all-to-all-start) | async-done | bytes 1966112 | tf_op jit(solution)/shard_map/all_to_all | solution.py:238
  140.8 1.3 copy-done.2
  142.1 4.7 %all-to-all-start.2 = ((f32[8,2,96,640]{3,2,1,0:T(8,128)}), f32[8,2,96,640]{3,2,1,0:T(8,128)}, u32[]{:S(2)}, u32[]{:S(2)}) async-start(f32[8,2,96,640]{3,2,1,0:T(8,128)} %pad_maximum_fusion), calls=%async_computation.2 | async-start | bytes 7864320 | tf_op jit(solution)/shard_map/all_to_all | solution.py:238
  146.8 0.2 add_divide_fusion.1
  147.0 1.8 copy.23
  148.8 2.3 reshape.110
  151.1 2.0 copy.24
  153.0 1.6 copy.25
  154.6 0.1 pad_maximum_fusion.3.kz_ref
  154.7 0.6 pad_maximum_fusion.1.fac_ref
  155.3 1.0 copy-done.3
  156.3 21.4 %spanwise_v.1 = f32[8,96,640]{2,1,0:T(8,128)S(1)} custom-call(f32[3,16]{1,0:T(4,128)S(1)} %copy-done.6, f32[1]{0:T(128)} %bitcast.flow_ref, f32[8,96,640]{2,1,0:T(8,128)S(1)} %bitcast.57, f32[8,640]{1,0:T(8,128)S(1)} %pad_maximum_fusion.3.kz_ref, f32[12,96,640]{2,1,0:T(8,128)S(1)} %pad_maximum_fusion.1.fac_ref, ...), custom_call_target="tpu_custom_call" | custom-call | flops 5662310400 | bytes 19660800 | tf_op jit(solution)/shard_map/spanwise_v/pallas_call | solution.py:147
  177.7 0.0 copy-start.4
  177.7 1.3 copy-done.4
  179.0 14.0 %all-to-all-done.2 = f32[8,2,96,640]{3,2,1,0:T(8,128)} async-done(((f32[8,2,96,640]{3,2,1,0:T(8,128)}), f32[8,2,96,640]{3,2,1,0:T(8,128)}, u32[]{:S(2)}, u32[]{:S(2)}) %all-to-all-start.2) | async-done | bytes 3932192 | tf_op jit(solution)/shard_map/all_to_all | solution.py:238
  192.9 4.3 %all-to-all-start.1 = ((f32[8,96,640]{2,1,0:T(8,128)}), f32[8,96,640]{2,1,0:T(8,128)}, u32[]{:S(2)}, u32[]{:S(2)}) async-start(f32[8,96,640]{2,1,0:T(8,128)} %copy-done.4), calls=%async_computation.1 | async-start | bytes 3932160 | tf_op jit(solution)/shard_map/all_to_all | solution.py:261
  197.3 34.4 %spanwise_omega.1 = f32[8,96,640]{2,1,0:T(8,128)S(1)} custom-call(f32[3,16]{1,0:T(4,128)S(1)} %copy-done.6, f32[1]{0:T(128)} %bitcast.flow_ref, f32[8,192,640]{2,1,0:T(8,128)} %bitcast.28.x_ref, f32[8,640]{1,0:T(8,128)S(1)} %pad_maximum_fusion.3.kz_ref, f32[12,96,640]{2,1,0:T(8,128)S(1)} %pad_maximum_fusion.1.fac_ref, ...), custom_call_target="tpu_custom_call" | custom-call | flops 11324620800 | bytes 19660800 | tf_op jit(solution)/shard_map/spanwise_omega/pallas_call | solution.py:147
  231.6 1.3 copy-done.5
  232.9 4.1 %all-to-all-start.3 = ((f32[8,96,640]{2,1,0:T(8,128)}), f32[8,96,640]{2,1,0:T(8,128)S(1)}, u32[]{:S(2)}, u32[]{:S(2)}) async-start(f32[8,96,640]{2,1,0:T(8,128)} %copy-done.5), calls=%async_computation.3 | async-start | bytes 3932160 | tf_op jit(solution)/shard_map/all_to_all | solution.py:261
  237.0 2.8 %copy.26 = f32[640,768]{1,0:T(8,128)} copy(f32[640,768]{0,1:T(8,128)} %bitcast.16) | data formatting | bytes 3932160 | tf_op jit(solution)/shard_map/transpose | solution.py:263
  239.8 22.4 %all-to-all-done.3 = f32[8,96,640]{2,1,0:T(8,128)S(1)} async-done(((f32[8,96,640]{2,1,0:T(8,128)}), f32[8,96,640]{2,1,0:T(8,128)S(1)}, u32[]{:S(2)}, u32[]{:S(2)}) %all-to-all-start.3) | async-done | bytes 1966112 | tf_op jit(solution)/shard_map/all_to_all | solution.py:261
  262.3 1.8 copy.29
  (30 shorter events, 0.1 us)
Async XLA Ops:
  7.2 1.3 copy-start
  7.2 53.9 %all-gather.8.cloned.1.call-start = ((), (), s32[]{:S(2)}) async-start(), calls=%async_computation.5 | async-start | bytes 2654208 | tf_op jit(solution)/shard_map/all_gather | solution.py:184
  9.4 24.2 %copy-start.15 = (f32[768]{0:T(1024)S(1)}, f32[768]{0:T(1024)}, u32[]{:S(2)}) copy-start(f32[768]{0:T(1024)} %param.13) | copy-start | bytes 9220
  32.5 69.4 %all-gather.6.cloned.1.call-start = ((), (), s32[]{:S(2)}) async-start(), calls=%async_computation.4 | async-start | bytes 5308416 | tf_op jit(solution)/shard_map/all_gather | solution.py:184
  33.6 3.1 %copy-start.8 = (f32[2,1,320,768]{3,2,1,0:T(8,128)S(1)}, f32[2,1,320,768]{3,2,1,0:T(8,128)}, u32[]{:S(2)}) copy-start(f32[2,1,320,768]{3,2,1,0:T(8,128)} %param.9) | copy-start | bytes 5898244
  61.1 6.7 %copy-start.7 = (f32[1,4,192,768]{3,2,1,0:T(8,128)S(1)}, f32[1,4,192,768]{3,2,1,0:T(8,128)}, u32[]{:S(2)}) copy-start(f32[1,4,192,768]{3,2,1,0:T(8,128)} %all-gather.8.cloned.1.call-done) | copy-start | bytes 7077892
  72.1 35.5 %copy-start.13 = (f32[768,640]{1,0:T(8,128)S(1)}, f32[768,640]{1,0:T(8,128)}, u32[]{:S(2)}) copy-start(f32[768,640]{1,0:T(8,128)} %fusion.41) | copy-start | bytes 5898244
  106.1 1.4 copy-start.10
  112.0 28.8 %all-to-all-start = ((f32[8,1,96,640]{3,2,1,0:T(8,128)}), f32[8,1,96,640]{3,2,1,0:T(8,128)S(1)}, u32[]{:S(2)}, u32[]{:S(2)}) async-start(f32[8,1,96,640]{3,2,1,0:T(8,128)} %fusion.15), calls=%async_computation | async-start | bytes 3932160 | tf_op jit(solution)/shard_map/all_to_all | solution.py:238
  115.8 5.1 %copy-start.11 = (f32[1,4,192,768]{3,2,1,0:T(8,128)S(1)}, f32[1,4,192,768]{3,2,1,0:T(8,128)}, u32[]{:S(2)}) copy-start(f32[1,4,192,768]{3,2,1,0:T(8,128)} %copy-done.10) | copy-start | bytes 7077892
  115.8 5.1 %copy-start.12 = (f32[768,640]{1,0:T(8,128)S(1)}, f32[768,640]{1,0:T(8,128)}, u32[]{:S(2)}) copy-start(f32[768,640]{1,0:T(8,128)} %fusion) | copy-start | bytes 5898244
  121.0 3.3 %copy-start.9 = (f32[1,4,192,768]{3,2,1,0:T(8,128)S(1)}, f32[1,4,192,768]{3,2,1,0:T(8,128)}, u32[]{:S(2)}) copy-start(f32[1,4,192,768]{3,2,1,0:T(8,128)} %get-tuple-element.2) | copy-start | bytes 7077892
  130.2 16.6 %copy-start.14 = (f32[96,3840]{1,0:T(8,128)S(1)}, f32[96,3840]{1,0:T(8,128)}, u32[]{:S(2)}) copy-start(f32[96,3840]{1,0:T(8,128)} %param.14) | copy-start | bytes 4423684
  140.8 1.3 copy-start.2
  142.1 50.8 %all-to-all-start.2 = ((f32[8,2,96,640]{3,2,1,0:T(8,128)}), f32[8,2,96,640]{3,2,1,0:T(8,128)}, u32[]{:S(2)}, u32[]{:S(2)}) async-start(f32[8,2,96,640]{3,2,1,0:T(8,128)} %pad_maximum_fusion), calls=%async_computation.2 | async-start | bytes 7864320 | tf_op jit(solution)/shard_map/all_to_all | solution.py:238
  154.7 1.5 copy-start.3
  154.7 1.5 copy-start.6
  177.7 1.3 copy-start.4
  192.9 40.0 %all-to-all-start.1 = ((f32[8,96,640]{2,1,0:T(8,128)}), f32[8,96,640]{2,1,0:T(8,128)}, u32[]{:S(2)}, u32[]{:S(2)}) async-start(f32[8,96,640]{2,1,0:T(8,128)} %copy-done.4), calls=%async_computation.1 | async-start | bytes 3932160 | tf_op jit(solution)/shard_map/all_to_all | solution.py:261
  231.6 1.3 copy-start.5
  232.9 29.3 %all-to-all-start.3 = ((f32[8,96,640]{2,1,0:T(8,128)}), f32[8,96,640]{2,1,0:T(8,128)S(1)}, u32[]{:S(2)}, u32[]{:S(2)}) async-start(f32[8,96,640]{2,1,0:T(8,128)} %copy-done.5), calls=%async_computation.3 | async-start | bytes 3932160 | tf_op jit(solution)/shard_map/all_to_all | solution.py:261
  262.2 1.8 copy-start.1
Sparse Core Ops, SparseCore 0:
  32.6 28.4 all-gather.7
  63.0 38.9 all-gather.5

commit v5 on v4

--- a/solution.py
+++ b/solution.py
@@ -184,7 +184,7 @@
         rows = lax.all_gather(part, "row", axis=2, tiled=False)
         return rows.reshape(part.shape[0], extent * lax.axis_size("col"), count_y)
 
-    return everyone(columns[:1])[0], everyone(columns[1:])
+    return everyone(columns[:1])[0], [everyone(columns[1:2])[0], everyone(columns[2:])[0]]
 
 
 def shards(source_v, source_omega, forward_map, back_maps, eigenvalues, penalty):

time: 272 us -> 276 us (1.015)
  local copies, waits for them, and re-layouts: 30.5 us -> 24.2 us
  matrix products: 27.6 us -> 33.7 us
  waiting for transfers between devices: 100 us -> 106 us
    all_gather x2 -> x3, waiting for transfers between devices: 53.2 us -> 67.6 us  [everyone(): rows = lax.all_gather(part, 'row', axis=2, tiled=False)]
    all_to_all x2, waiting for transfers between devices: 24.6 us -> 14.2 us  [sent(): data = lax.all_to_all(fields, 'row', split_axis=0, concat_axis=0)]
    dot_general x3, matrix products: 11.5 us -> 18 us  [back_of(): return jnp.einsum('yj,jk->yk', back[which], coeffs, precision=HIGH)]
    slice x3 -> x1, local copies, waits for them, and re-layouts: 5.8 us -> 0.93 us  [gather_maps(): columns[2:]]
    unnamed x32 -> x26, local copies, waits for them, and re-layouts: 7.48 us -> 6.05 us
  transfers between devices with their start and end apart: 6 -> 7, of which waited for: 5 -> 5; matrix products, arithmetic and copies ran while one was open for 15% -> 19% of each run, Pallas kernels for 21% -> 20%
where the time goes in v5:
time: 276 us
  waiting for transfers between devices  106 us (38%)
  Pallas kernels  55.8 us (20%)
  matrix products  33.7 us (12%)
  local copies, waits for them, and re-layouts  24.2 us (9%)
  blocking collectives  22.4 us (8%)
  starting transfers between devices  16.8 us (6%)
  between operations  14 us (5%)
  other arithmetic  3.12 us (1%)
    all_gather x3, waiting for transfers between devices, everyone(): rows = lax.all_gather(part, 'row', axis=2, tiled=False)  67.6 us
    pallas_call x2, Pallas kernels, spanwise_pass(): pl.pallas_call(spanwise_kernel, grid=(3, 4), out_shape=jax.ShapeDtypeStru...  55.8 us
    all_to_all x2, waiting for transfers between devices, finished(): returned = lax.all_to_all(result, 'row', split_axis=0, concat_axis=0)  22.4 us
    all_gather x1, blocking collectives, gather_maps(): lax.all_gather(jnp.concatenate(own, axis=0), 'col', axis=1, tiled=False)  22.4 us
    dot_general x3, matrix products, back_of(): return jnp.einsum('yj,jk->yk', back[which], coeffs, precision=HIGH)  18 us
    dot_general x3, matrix products, coefficients(): return jnp.einsum('jn,kn->jk', forward, rows, precision=HIGH) * scaling  15.7 us
    all_to_all x2, waiting for transfers between devices, sent(): data = lax.all_to_all(fields, 'row', split_axis=0, concat_axis=0)  14.2 us
    all_to_all x2, starting transfers between devices, finished(): returned = lax.all_to_all(result, 'row', split_axis=0, concat_axis=0)  8.41 us
  transfers between devices with their start and end apart: 7, of which 5 were waited for; matrix products, arithmetic and copies ran while one was open for 19% of the time, Pallas kernels for 20%

profile of v5, /device:TPU:0, one launch (start us, length us, event | category | flops | bytes accessed | tf_op | source)
XLA Modules:
  0.0 275.7 jit_solution(3382306546313287458)
XLA Ops:
  7.2 0.0 copy-start
  7.2 0.0 all-gather.10.cloned.1.call-start
  7.2 1.2 copy-done
  8.5 0.9 dynamic-slice_bitcast_fusion
  9.4 0.0 copy-start.11
  9.4 22.4 %all-gather = f32[3,96,768]{2,1,0:T(8,128)S(1)} all-gather(f32[3,24,768]{2,1,0:T(8,128)S(1)} %pad_maximum_fusion.2), channel_id=2, replica_groups=mesh['row'=8,'col'=4] {'col'}, dimensions={1}, use_global_device_ids=true | all-gather | bytes 1105920 | tf_op jit(solution)/shard_map/all_gather | solution.py:181
  31.8 0.9 fusion.40
  32.7 0.0 all-gather.10.cloned.1.call-update
  32.7 0.0 all-gather.8.cloned.1.call-start
  32.8 0.7 all-gather.8.cloned.1.call-update
  33.5 0.0 all-gather.12.cloned.1.call-start
  33.5 0.7 all-gather.12.cloned.1.call-update
  34.2 0.1 pad_maximum_fusion.4
  34.3 3.1 %slice_bitcast_fusion.3 = (f32[320,768]{1,0:T(8,128)}, f32[320,768]{1,0:T(8,128)}) fusion(f32[2,1,320,768]{3,2,1,0:T(8,128)} %param.10), kind=kLoop, calls=%fused_computation.25 | loop fusion | bytes 3932160 | tf_op jit(solution)/shard_map/squeeze | solution.py:217
  37.4 1.1 slice_bitcast_fusion.1
  38.5 22.7 %all-gather.10.cloned.1.call-done = f32[1,4,192,768]{3,2,1,0:T(8,128)} async-done(((f32[1,4,24,768]{3,2,1,0:T(8,128)}), f32[1,4,192,768]{3,2,1,0:T(8,128)}) %all-gather.10.cloned.1.call-update) | async-done | bytes 2359312 | tf_op jit(solution)/shard_map/all_gather | solution.py:184
  61.3 6.0 %fusion.41 = f32[768,640]{1,0:T(8,128)} fusion(f32[768,768]{1,0:T(8,128)} %bitcast.59, f32[640,768]{1,0:T(8,128)S(1)} %bitcast.63), kind=kOutput, calls=%fused_computation.59 | convolution fusion | flops 2264924160 | bytes 6291456 | tf_op jit(solution)/shard_map/jn,kn->jk/dot_general | solution.py:220
  67.3 25.6 %all-gather.8.cloned.1.call-done = f32[1,4,192,768]{3,2,1,0:T(8,128)} async-done(((f32[1,4,24,768]{3,2,1,0:T(8,128)}), f32[1,4,192,768]{3,2,1,0:T(8,128)}) %all-gather.8.cloned.1.call-update) | async-done | bytes 2359312 | tf_op jit(solution)/shard_map/all_gather | solution.py:184
  92.8 6.8 %fusion.15 = f32[8,1,96,640]{3,2,1,0:T(8,128)} fusion(f32[8,96,768]{2,1,0:T(8,128)} %bitcast.74, f32[768,640]{1,0:T(8,128)} %fusion.41, f32[640]{0:T(1024)S(1)} %get-tuple-element.12, f32[768]{0:T(1024)S(1)} %broadcast_add_fusion), kind=kOutput, calls=%fused_computation.20 | convolution fusion | flops 2266398720 | bytes 6297088 | tf_op jit(solution)/shard_map/yj,jk->yk/dot_general | solution.py:223
  99.6 3.8 %all-to-all-start = ((f32[8,1,96,640]{3,2,1,0:T(8,128)}), f32[8,1,96,640]{3,2,1,0:T(8,128)S(1)}, u32[]{:S(2)}, u32[]{:S(2)}) async-start(f32[8,1,96,640]{3,2,1,0:T(8,128)} %fusion.15), calls=%async_computation | async-start | bytes 3932160 | tf_op jit(solution)/shard_map/all_to_all | solution.py:238
  103.4 5.4 %fusion = f32[768,640]{1,0:T(8,128)S(1)} fusion(f32[768,768]{1,0:T(8,128)} %bitcast.60, f32[320,768]{1,0:T(8,128)} %get-tuple-element.7, f32[320,768]{1,0:T(8,128)} %get-tuple-element.6), kind=kOutput, calls=%fused_computation.2 | convolution fusion | flops 2265415680 | bytes 6291456 | tf_op jit(solution)/shard_map/jn,kn->jk/dot_general | solution.py:220
  108.8 4.4 %fusion.4 = f32[768,640]{1,0:T(8,128)} fusion(f32[768,768]{1,0:T(8,128)S(1)} %bitcast.61, f32[320,768]{1,0:T(8,128)S(1)} %copy-done.9, f32[320,768]{1,0:T(8,128)S(1)} %get-tuple-element.4), kind=kOutput, calls=%fused_computation.6 | convolution fusion | flops 2265415680 | bytes 6291456 | tf_op jit(solution)/shard_map/jn,kn->jk/dot_general | solution.py:220
  113.2 4.5 %fusion.12 = f32[768,640]{1,0:T(8,128)} fusion(f32[768,768]{1,0:T(8,128)S(1)} %bitcast.75, f32[768,640]{1,0:T(8,128)S(1)} %fusion, f32[640]{0:T(1024)S(1)} %get-tuple-element.12, f32[768]{0:T(1024)S(1)} %broadcast_add_fusion), kind=kOutput, calls=%fused_computation.16 | convolution fusion | flops 2266398720 | bytes 6297088 | tf_op jit(solution)/shard_map/yj,jk->yk/dot_general | solution.py:223
  117.7 19.3 %all-gather.12.cloned.1.call-done = f32[1,4,192,768]{3,2,1,0:T(8,128)} async-done(((f32[1,4,24,768]{3,2,1,0:T(8,128)}), f32[1,4,192,768]{3,2,1,0:T(8,128)}) %all-gather.12.cloned.1.call-update) | async-done | bytes 2359312 | tf_op jit(solution)/shard_map/all_gather | solution.py:184
  137.0 6.7 %multiply_divide_fusion.1 = (f32[768,640]{1,0:T(8,128)S(1)}, f32[768,640]{1,0:T(8,128)S(1)}) fusion(f32[768,640]{1,0:T(8,128)} %fusion.12, f32[640]{0:T(1024)S(1)} %get-tuple-element.13, f32[]{:T(128)} %mul_shard_map.3, f32[640]{0:T(1024)S(1)} %get-tuple-element.11, f32[640]{0:T(1024)S(1)} %get-tuple-element.14, f32[640]{0:T(1024)S(1)} %fusion.34, ...), kind=kOutput, calls=%fused_computation.13 | convolution fusion | flops 2271313920 | bytes 10239492 | tf_op jit(solution)/shard_map/yj,jk->yk/dot_general | solution.py:223
  143.7 2.2 pad_maximum_fusion
  145.9 0.0 all-to-all-done
  145.9 1.3 copy-done.2
  147.2 4.5 %all-to-all-start.2 = ((f32[8,2,96,640]{3,2,1,0:T(8,128)}), f32[8,2,96,640]{3,2,1,0:T(8,128)}, u32[]{:S(2)}, u32[]{:S(2)}) async-start(f32[8,2,96,640]{3,2,1,0:T(8,128)} %pad_maximum_fusion), calls=%async_computation.2 | async-start | bytes 7864320 | tf_op jit(solution)/shard_map/all_to_all | solution.py:238
  151.7 0.2 add_divide_fusion.1
  151.9 1.8 copy.23
  153.7 2.3 reshape.105
  155.9 2.0 copy.24
  157.9 1.6 copy.25
  159.5 0.1 pad_maximum_fusion.3.kz_ref
  159.6 0.6 pad_maximum_fusion.1.fac_ref
  160.2 1.0 copy-done.3
  161.1 21.4 %spanwise_v.1 = f32[8,96,640]{2,1,0:T(8,128)S(1)} custom-call(f32[3,16]{1,0:T(4,128)S(1)} %copy-done.6, f32[1]{0:T(128)} %bitcast.flow_ref, f32[8,96,640]{2,1,0:T(8,128)S(1)} %bitcast.58, f32[8,640]{1,0:T(8,128)S(1)} %pad_maximum_fusion.3.kz_ref, f32[12,96,640]{2,1,0:T(8,128)S(1)} %pad_maximum_fusion.1.fac_ref, ...), custom_call_target="tpu_custom_call" | custom-call | flops 5662310400 | bytes 19660800 | tf_op jit(solution)/shard_map/spanwise_v/pallas_call | solution.py:147
  182.6 0.0 copy-start.4
  182.6 1.3 copy-done.4
  183.9 14.2 %all-to-all-done.2 = f32[8,2,96,640]{3,2,1,0:T(8,128)} async-done(((f32[8,2,96,640]{3,2,1,0:T(8,128)}), f32[8,2,96,640]{3,2,1,0:T(8,128)}, u32[]{:S(2)}, u32[]{:S(2)}) %all-to-all-start.2) | async-done | bytes 3932192 | tf_op jit(solution)/shard_map/all_to_all | solution.py:238
  198.0 4.3 %all-to-all-start.1 = ((f32[8,96,640]{2,1,0:T(8,128)}), f32[8,96,640]{2,1,0:T(8,128)}, u32[]{:S(2)}, u32[]{:S(2)}) async-start(f32[8,96,640]{2,1,0:T(8,128)} %copy-done.4), calls=%async_computation.1 | async-start | bytes 3932160 | tf_op jit(solution)/shard_map/all_to_all | solution.py:261
  202.4 34.4 %spanwise_omega.1 = f32[8,96,640]{2,1,0:T(8,128)S(1)} custom-call(f32[3,16]{1,0:T(4,128)S(1)} %copy-done.6, f32[1]{0:T(128)} %bitcast.flow_ref, f32[8,192,640]{2,1,0:T(8,128)} %bitcast.29.x_ref, f32[8,640]{1,0:T(8,128)S(1)} %pad_maximum_fusion.3.kz_ref, f32[12,96,640]{2,1,0:T(8,128)S(1)} %pad_maximum_fusion.1.fac_ref, ...), custom_call_target="tpu_custom_call" | custom-call | flops 11324620800 | bytes 19660800 | tf_op jit(solution)/shard_map/spanwise_omega/pallas_call | solution.py:147
  236.7 1.3 copy-done.5
  238.0 4.1 %all-to-all-start.3 = ((f32[8,96,640]{2,1,0:T(8,128)}), f32[8,96,640]{2,1,0:T(8,128)S(1)}, u32[]{:S(2)}, u32[]{:S(2)}) async-start(f32[8,96,640]{2,1,0:T(8,128)} %copy-done.5), calls=%async_computation.3 | async-start | bytes 3932160 | tf_op jit(solution)/shard_map/all_to_all | solution.py:261
  242.1 2.8 %copy.26 = f32[640,768]{1,0:T(8,128)} copy(f32[640,768]{0,1:T(8,128)} %bitcast.16) | data formatting | bytes 3932160 | tf_op jit(solution)/shard_map/transpose | solution.py:263
  244.9 22.4 %all-to-all-done.3 = f32[8,96,640]{2,1,0:T(8,128)S(1)} async-done(((f32[8,96,640]{2,1,0:T(8,128)}), f32[8,96,640]{2,1,0:T(8,128)S(1)}, u32[]{:S(2)}, u32[]{:S(2)}) %all-to-all-start.3) | async-done | bytes 1966112 | tf_op jit(solution)/shard_map/all_to_all | solution.py:261
  267.4 1.8 copy.29
  (25 shorter events, 0.1 us)
Async XLA Ops:
  7.2 1.3 copy-start
  7.2 54.1 %all-gather.10.cloned.1.call-start = ((), (), s32[]{:S(2)}) async-start(), calls=%async_computation.5 | async-start | bytes 2654208 | tf_op jit(solution)/shard_map/all_gather | solution.py:184
  9.4 25.0 %copy-start.11 = (f32[768]{0:T(1024)S(1)}, f32[768]{0:T(1024)}, u32[]{:S(2)}) copy-start(f32[768]{0:T(1024)} %param.13) | copy-start | bytes 9220
  32.7 60.1 %all-gather.8.cloned.1.call-start = ((), (), s32[]{:S(2)}) async-start(), calls=%async_computation.4 | async-start | bytes 2654208 | tf_op jit(solution)/shard_map/all_gather | solution.py:184
  33.5 103.6 %all-gather.12.cloned.1.call-start = ((), (), s32[]{:S(2)}) async-start(), calls=%async_computation.6 | async-start | bytes 2654208 | tf_op jit(solution)/shard_map/all_gather | solution.py:184
  34.3 3.1 %copy-start.8 = (f32[2,1,320,768]{3,2,1,0:T(8,128)S(1)}, f32[2,1,320,768]{3,2,1,0:T(8,128)}, u32[]{:S(2)}) copy-start(f32[2,1,320,768]{3,2,1,0:T(8,128)} %param.9) | copy-start | bytes 5898244
  99.6 46.3 %all-to-all-start = ((f32[8,1,96,640]{3,2,1,0:T(8,128)}), f32[8,1,96,640]{3,2,1,0:T(8,128)S(1)}, u32[]{:S(2)}, u32[]{:S(2)}) async-start(f32[8,1,96,640]{3,2,1,0:T(8,128)} %fusion.15), calls=%async_computation | async-start | bytes 3932160 | tf_op jit(solution)/shard_map/all_to_all | solution.py:238
  103.4 5.4 %copy-start.7 = (f32[1,4,192,768]{3,2,1,0:T(8,128)S(1)}, f32[1,4,192,768]{3,2,1,0:T(8,128)}, u32[]{:S(2)}) copy-start(f32[1,4,192,768]{3,2,1,0:T(8,128)} %all-gather.10.cloned.1.call-done) | copy-start | bytes 7077892
  103.4 5.4 %copy-start.9 = (f32[320,768]{1,0:T(8,128)S(1)}, f32[320,768]{1,0:T(8,128)}, u32[]{:S(2)}) copy-start(f32[320,768]{1,0:T(8,128)} %get-tuple-element.5) | copy-start | bytes 2949124
  108.8 4.4 %copy-start.12 = (f32[1,4,192,768]{3,2,1,0:T(8,128)S(1)}, f32[1,4,192,768]{3,2,1,0:T(8,128)}, u32[]{:S(2)}) copy-start(f32[1,4,192,768]{3,2,1,0:T(8,128)} %all-gather.8.cloned.1.call-done) | copy-start | bytes 7077892
  145.9 5.8 %copy-start.10 = (f32[96,3840]{1,0:T(8,128)S(1)}, f32[96,3840]{1,0:T(8,128)}, u32[]{:S(2)}) copy-start(f32[96,3840]{1,0:T(8,128)} %param.14) | copy-start | bytes 4423684
  145.9 1.3 copy-start.2
  147.2 50.8 %all-to-all-start.2 = ((f32[8,2,96,640]{3,2,1,0:T(8,128)}), f32[8,2,96,640]{3,2,1,0:T(8,128)}, u32[]{:S(2)}, u32[]{:S(2)}) async-start(f32[8,2,96,640]{3,2,1,0:T(8,128)} %pad_maximum_fusion), calls=%async_computation.2 | async-start | bytes 7864320 | tf_op jit(solution)/shard_map/all_to_all | solution.py:238
  159.6 1.5 copy-start.3
  159.6 1.5 copy-start.6
  182.6 1.3 copy-start.4
  198.0 40.0 %all-to-all-start.1 = ((f32[8,96,640]{2,1,0:T(8,128)}), f32[8,96,640]{2,1,0:T(8,128)}, u32[]{:S(2)}, u32[]{:S(2)}) async-start(f32[8,96,640]{2,1,0:T(8,128)} %copy-done.4), calls=%async_computation.1 | async-start | bytes 3932160 | tf_op jit(solution)/shard_map/all_to_all | solution.py:261
  236.7 1.3 copy-start.5
  238.0 29.3 %all-to-all-start.3 = ((f32[8,96,640]{2,1,0:T(8,128)}), f32[8,96,640]{2,1,0:T(8,128)S(1)}, u32[]{:S(2)}, u32[]{:S(2)}) async-start(f32[8,96,640]{2,1,0:T(8,128)} %copy-done.5), calls=%async_computation.3 | async-start | bytes 3932160 | tf_op jit(solution)/shard_map/all_to_all | solution.py:261
  267.3 1.8 copy-start.1
Sparse Core Ops, SparseCore 0:
  32.8 28.4 all-gather.9
  63.8 29.0 all-gather.7
  94.7 42.2 all-gather.11
